TPU v7x, 32 devices: a whole 2x2x4 slice. The times are simulated.
32 devices in a mesh: groups: 2 (over y), leaf: 8 (over z, x), sub: 2 (over core).
Axes of the slice: x: 2, y: 2, z: 4, core: 2. Of those that a mesh axis runs over, the one named last changes fastest.
Arguments:
- multipoles: bfloat16 [8192, 64], P(('groups', 'leaf', 'sub')), parts along dimension 0, may hold values from -6 to 6
- list_src: int32 [8192, 189], P(('groups', 'leaf', 'sub')), parts along dimension 0, may hold values from 0 to 639, as said below
- list_mask: int32 [8192, 189], P(('groups', 'leaf', 'sub')), parts along dimension 0, may hold values 0 or 1
- send_boxes: int32 [32, 8, 16], P(('groups', 'leaf', 'sub')), parts along dimension 0, may hold values from 0 to 255
- send_count: int32 [32, 8], P(('groups', 'leaf', 'sub')), parts along dimension 0, may hold values from 0 to 16, as said below
- coarse_src: int32 [128, 189], P(('groups', 'leaf', 'sub')), parts along dimension 0, may hold values from 0 to 63
- coarse_mask: int32 [128, 189], P(('groups', 'leaf', 'sub')), parts along dimension 0, may hold values 0 or 1
- m2l_ops: bfloat16 [316, 64, 64], replicated, may hold values from -0.0546875 to 0.0546875
- m2m_ops: float32 [8, 64, 64], replicated, may hold values from -0.25 to 0.25
- l2l_ops: float32 [8, 64, 64], replicated, may hold values from -0.75 to 0.75
Outputs:
- leaf_locals: float32 [8192, 64], P(('groups', 'leaf', 'sub')), parts along dimension 0
There are 2 independent parts, one for each index of `groups`. A program takes and returns all parts, laid end to end along the dimension named above; an argument that names none is the same for every part. Nothing has to cross between parts.
Inputs may be any that keep to these rules, and one draw needn't show every extreme that they name: `list_src`: an entry e at or above 512 names a leaf index (e - 512) // 16 that differs from the target device's own leaf index in exactly one bit, and a slot below that sender's count toward the target's leaf index. `send_count`: nonzero exactly toward the leaf indices that differ from the sender's own leaf index in one bit; each sender has 16 toward at least one of them.
All inputs are finite; a program needn't handle non-finite values. No bound on the sum of `list_mask` or of `coarse_mask` on one device may be relied on, other than what follows from the above.
Results may differ from a plain program's by a relative error of at most 0.0022.
Values may be sent and summed in bfloat16 or wider, within the bound.
A program may use at most 128 MiB of HBM per device.

v0:
```python
import jax
import jax.numpy as jnp
import numpy as np
from jax import lax
from jax.sharding import PartitionSpec as P

LEVELS = 2


def offset_tables():
    vector_rank = {}
    counter = 0
    for step_x in range(-3, 4):
        for step_y in range(-3, 4):
            for step_z in range(-3, 4):
                if max(abs(step_x), abs(step_y), abs(step_z)) > 1:
                    vector_rank[step_x, step_y, step_z] = counter
                    counter += 1
    vector_table = []
    for octant in range(8):
        shifts = [octant >> position & 1 for position in range(3)]
        entries = []
        for step_x in range(-2 - shifts[0], 4 - shifts[0]):
            for step_y in range(-2 - shifts[1], 4 - shifts[1]):
                for step_z in range(-2 - shifts[2], 4 - shifts[2]):
                    if max(abs(step_x), abs(step_y), abs(step_z)) > 1:
                        entries.append(vector_rank[step_x, step_y, step_z])
        vector_table.append(entries)
    return np.array(vector_table, dtype=np.int32)


def far_field(table_rows, sources, weights, m2l_ops, coeffs):
    vectors = offset_tables()
    count_targets = sources.shape[0]
    grouped_src = sources.reshape(count_targets // 8, 8, -1)
    grouped_wts = weights.reshape(count_targets // 8, 8, -1)
    results = []
    for octant in range(8):
        picked = jnp.take(table_rows, grouped_src[:, octant], axis=0)
        picked = jnp.where(grouped_wts[:, octant, :, None] > 0, picked, jnp.zeros((), picked.dtype))
        flat_ops = jnp.take(m2l_ops, jnp.asarray(vectors[octant]), axis=0).reshape(-1, coeffs)
        results.append(
            jnp.dot(
                picked.reshape(picked.shape[0], -1), flat_ops, preferred_element_type=jnp.float32
            )
        )
    return jnp.stack(results, axis=1).reshape(count_targets, coeffs)


def upward(children, m2m_ops):
    grouped = children.reshape(-1, 8, children.shape[-1])
    return jnp.einsum("noc,ocd->nd", grouped, m2m_ops, precision=lax.Precision.HIGHEST)


def downward(parents, l2l_ops):
    spread = jnp.einsum("nc,ocd->nod", parents, l2l_ops, precision=lax.Precision.HIGHEST)
    return spread.reshape(-1, parents.shape[-1])


def per_device(
    multipoles,
    list_src,
    list_mask,
    send_boxes,
    send_count,
    coarse_src,
    coarse_mask,
    m2l_ops,
    m2m_ops,
    l2l_ops,
):
    coeffs = multipoles.shape[1]
    count_leaf = lax.axis_size("leaf")
    capacity = send_boxes.shape[2]
    slot_index = jnp.arange(capacity, dtype=jnp.int32)
    nothing = jnp.zeros((), multipoles.dtype)
    chip_rows = lax.all_gather(multipoles, "sub", axis=0, tiled=True)
    picked = jnp.take(multipoles, send_boxes[0], axis=0)
    live = slot_index[None, :] < send_count[0][:, None]
    outgoing = jnp.where(live[:, :, None], picked, nothing).reshape(count_leaf, capacity * coeffs)
    incoming = lax.all_to_all(outgoing, "leaf", split_axis=0, concat_axis=0, tiled=True)
    table_rows = jnp.concatenate([chip_rows, incoming.reshape(-1, coeffs)], axis=0)
    far_leaf = far_field(table_rows, list_src, list_mask, m2l_ops, coeffs)
    current = multipoles.astype(jnp.float32)
    for level_step in range(LEVELS):
        current = upward(current, m2m_ops)
    coarse_rows = current.astype(jnp.bfloat16)
    all_coarse = lax.all_gather(coarse_rows, ("leaf", "sub"), axis=0, tiled=True)
    count_coarse = coarse_rows.shape[0]
    first_coarse = lax.axis_index(("leaf", "sub")) * count_coarse
    octants = (first_coarse + jnp.arange(count_coarse, dtype=jnp.int32)) % 8
    vector_ids = jnp.take(jnp.asarray(offset_tables()), octants, axis=0)
    coarse_ops = jnp.take(m2l_ops, vector_ids, axis=0)
    coarse_picked = jnp.take(all_coarse, coarse_src, axis=0)
    coarse_picked = jnp.where(coarse_mask[:, :, None] > 0, coarse_picked, nothing)
    inherited = jnp.einsum(
        "jkc,jkcd->jd", coarse_picked, coarse_ops, preferred_element_type=jnp.float32
    )
    for level_step in range(LEVELS):
        inherited = downward(inherited, l2l_ops)
    return far_leaf + inherited


def solution(mesh):
    placed = (
        P(("groups", "leaf", "sub"), None),
        P(("groups", "leaf", "sub"), None),
        P(("groups", "leaf", "sub"), None),
        P(("groups", "leaf", "sub"), None, None),
        P(("groups", "leaf", "sub"), None),
        P(("groups", "leaf", "sub"), None),
        P(("groups", "leaf", "sub"), None),
        P(),
        P(),
        P(),
    )
    return jax.shard_map(
        per_device,
        mesh=mesh,
        in_specs=placed,
        out_specs=P(("groups", "leaf", "sub"), None),
        check_vma=False,
    )
```

profile of v0, /device:TPU:0, one launch (start us, length us, event | category | flops | bytes accessed | tf_op | source)
XLA Modules:
  0.0 361.0 jit_solution(5910559717525410181)
XLA Ops:
  6.0 7.3 %all-to-all-start = ((bf16[8,2,512]{2,1,0:T(2,128)(2,1)}), bf16[8,2,512]{2,1,0:T(2,128)(2,1)S(1)}, u32[]{:S(2)}, u32[]{:S(2)}) async-start(bf16[8,2,512]{2,1,0:T(2,128)(2,1)} %reshape.575), calls=%async_computation | async-start | bytes 32768 | tf_op jit(solution)/shard_map/all_to_all | solution.py:81
  19.0 10.1 %copy.122 = bf16[316,64,64]{2,1,0:T(8,128)(2,1)} copy(bf16[316,64,64]{0,2,1:T(8,128)(2,1)} %param.30) | data formatting | bytes 5177344 | tf_op args[7]
  30.5 22.0 %all-gather = bf16[16,4,64]{2,1,0:T(4,128)(2,1)S(1)} all-gather(bf16[1,4,64]{2,1,0:T(4,128)(2,1)S(1)} %fusion.67), channel_id=1, replica_groups=mesh['groups'=2,'leaf'=8,'sub'=2] {'leaf','sub'}, dimensions={0}, use_global_device_ids=true | all-gather | bytes 8704 | tf_op jit(solution)/shard_map/all_gather | solution.py:88
  55.2 21.5 %gather_fusion.3 = bf16[756,64,64]{2,1,0:T(8,128)(2,1)} fusion(bf16[316,64,64]{2,1,0:T(8,128)(2,1)} %copy.122, s32[1024]{0:T(1024)S(1)} %get-tuple-element.31), kind=kCustom, calls=%fused_computation.19 | custom fusion | bytes 12389328 | tf_op jit(solution)/shard_map/jit(_take)/gather | solution.py:93
  76.7 7.1 %broadcast_select_fusion = bf16[4,189,64,64]{3,2,1,0:T(8,128)(2,1)S(1)} fusion(bf16[4,189,64,64]{3,2,1,0:T(8,128)(2,1)} %bitcast.167, pred[4,189]{1,0:T(4,128)(4,1)S(1)} %compare_and_fusion.8), kind=kLoop, calls=%fused_computation.22 | loop fusion | flops 3096576 | bytes 12387060 | tf_op jit(solution)/shard_map/jit(_take)/select_n | solution.py:93
  83.9 12.8 %fusion = f32[4,1,64,1]{2,1,3,0:T(1,128)S(1)} fusion(bf16[4,189,64,64]{3,2,1,0:T(8,128)(2,1)S(1)} %broadcast_select_fusion, bf16[4,189,64,1]{1,0,2,3:T(4,128)(2,1)S(1)} %select_bitcast_fusion), kind=kOutput, calls=%fused_computation.20 | convolution fusion | flops 6193152 | bytes 6290944 | tf_op jit(solution)/shard_map/jkc,jkcd->jd/dot_general | solution.py:96
  97.0 5.2 %gather_fusion.5 = bf16[189,64,64]{2,1,0:T(8,128)(2,1)} fusion(bf16[316,64,64]{2,1,0:T(8,128)(2,1)} %copy.122, s32[1024]{0:T(1024)S(1)} %get-tuple-element.39), kind=kCustom, calls=%fused_computation.1.clone | custom fusion | bytes 3097332 | tf_op jit(solution)/shard_map/jit(_take)/gather | solution.py:41
  102.2 5.2 %gather_fusion.7 = bf16[189,64,64]{2,1,0:T(8,128)(2,1)} fusion(bf16[316,64,64]{2,1,0:T(8,128)(2,1)} %copy.122, s32[1024]{0:T(1024)S(1)} %get-tuple-element.38), kind=kCustom, calls=%fused_computation.9.clone | custom fusion | bytes 3097332 | tf_op jit(solution)/shard_map/jit(_take)/gather | solution.py:41
  107.4 5.2 %gather_fusion.9 = bf16[189,64,64]{2,1,0:T(8,128)(2,1)} fusion(bf16[316,64,64]{2,1,0:T(8,128)(2,1)} %copy.122, s32[1024]{0:T(1024)S(1)} %get-tuple-element.37), kind=kCustom, calls=%fused_computation.10.clone | custom fusion | bytes 3097332 | tf_op jit(solution)/shard_map/jit(_take)/gather | solution.py:41
  112.5 5.2 %gather_fusion.11 = bf16[189,64,64]{2,1,0:T(8,128)(2,1)} fusion(bf16[316,64,64]{2,1,0:T(8,128)(2,1)} %copy.122, s32[1024]{0:T(1024)S(1)} %get-tuple-element.36), kind=kCustom, calls=%fused_computation.11.clone | custom fusion | bytes 3097332 | tf_op jit(solution)/shard_map/jit(_take)/gather | solution.py:41
  117.7 5.2 %gather_fusion.13 = bf16[189,64,64]{2,1,0:T(8,128)(2,1)} fusion(bf16[316,64,64]{2,1,0:T(8,128)(2,1)} %copy.122, s32[1024]{0:T(1024)S(1)} %get-tuple-element.35), kind=kCustom, calls=%fused_computation.12.clone | custom fusion | bytes 3097332 | tf_op jit(solution)/shard_map/jit(_take)/gather | solution.py:41
  122.9 5.2 %gather_fusion.15 = bf16[189,64,64]{2,1,0:T(8,128)(2,1)} fusion(bf16[316,64,64]{2,1,0:T(8,128)(2,1)} %copy.122, s32[1024]{0:T(1024)S(1)} %get-tuple-element.34), kind=kCustom, calls=%fused_computation.13.clone | custom fusion | bytes 3097332 | tf_op jit(solution)/shard_map/jit(_take)/gather | solution.py:41
  128.1 5.2 %gather_fusion.17 = bf16[189,64,64]{2,1,0:T(8,128)(2,1)} fusion(bf16[316,64,64]{2,1,0:T(8,128)(2,1)} %copy.122, s32[1024]{0:T(1024)S(1)} %get-tuple-element.33), kind=kCustom, calls=%fused_computation.14.clone | custom fusion | bytes 3097332 | tf_op jit(solution)/shard_map/jit(_take)/gather | solution.py:41
  133.3 5.1 %gather_fusion.19 = bf16[189,64,64]{2,1,0:T(8,128)(2,1)} fusion(bf16[316,64,64]{2,1,0:T(8,128)(2,1)} %copy.122, s32[1024]{0:T(1024)S(1)} %get-tuple-element.32), kind=kCustom, calls=%fused_computation.15.clone | custom fusion | bytes 3097332 | tf_op jit(solution)/shard_map/jit(_take)/gather | solution.py:41
  138.7 18.4 %gather_fusion.4 = bf16[6048,64]{1,0:T(8,128)(2,1)S(1)} fusion(bf16[640,64]{1,0:T(8,128)(2,1)S(1)} %constant_dynamic-update-slice_fusion, s32[6144]{0:T(1024)S(1)} %get-tuple-element.30), kind=kCustom, calls=%fused_computation.clone | custom fusion | bytes 1572480 | tf_op jit(solution)/shard_map/jit(_take)/gather | solution.py:39
  162.4 18.4 %gather_fusion.6 = bf16[6048,64]{1,0:T(8,128)(2,1)S(1)} fusion(bf16[640,64]{1,0:T(8,128)(2,1)S(1)} %constant_dynamic-update-slice_fusion, s32[6144]{0:T(1024)S(1)} %get-tuple-element.29), kind=kCustom, calls=%fused_computation.2.clone | custom fusion | bytes 1572480 | tf_op jit(solution)/shard_map/jit(_take)/gather | solution.py:39
  186.1 18.4 %gather_fusion.8 = bf16[6048,64]{1,0:T(8,128)(2,1)S(1)} fusion(bf16[640,64]{1,0:T(8,128)(2,1)S(1)} %constant_dynamic-update-slice_fusion, s32[6144]{0:T(1024)S(1)} %get-tuple-element.28), kind=kCustom, calls=%fused_computation.3.clone | custom fusion | bytes 1572480 | tf_op jit(solution)/shard_map/jit(_take)/gather | solution.py:39
  210.1 18.4 %gather_fusion.10 = bf16[6048,64]{1,0:T(8,128)(2,1)S(1)} fusion(bf16[640,64]{1,0:T(8,128)(2,1)S(1)} %constant_dynamic-update-slice_fusion, s32[6144]{0:T(1024)S(1)} %get-tuple-element.27), kind=kCustom, calls=%fused_computation.4.clone | custom fusion | bytes 1572480 | tf_op jit(solution)/shard_map/jit(_take)/gather | solution.py:39
  233.9 18.4 %gather_fusion.12 = bf16[6048,64]{1,0:T(8,128)(2,1)S(1)} fusion(bf16[640,64]{1,0:T(8,128)(2,1)S(1)} %constant_dynamic-update-slice_fusion, s32[6144]{0:T(1024)S(1)} %get-tuple-element.26), kind=kCustom, calls=%fused_computation.5.clone | custom fusion | bytes 1572480 | tf_op jit(solution)/shard_map/jit(_take)/gather | solution.py:39
  257.6 18.4 %gather_fusion.14 = bf16[6048,64]{1,0:T(8,128)(2,1)S(1)} fusion(bf16[640,64]{1,0:T(8,128)(2,1)S(1)} %constant_dynamic-update-slice_fusion, s32[6144]{0:T(1024)S(1)} %get-tuple-element.25), kind=kCustom, calls=%fused_computation.6.clone | custom fusion | bytes 1572480 | tf_op jit(solution)/shard_map/jit(_take)/gather | solution.py:39
  281.3 18.4 %gather_fusion.16 = bf16[6048,64]{1,0:T(8,128)(2,1)S(1)} fusion(bf16[640,64]{1,0:T(8,128)(2,1)S(1)} %constant_dynamic-update-slice_fusion, s32[6144]{0:T(1024)S(1)} %get-tuple-element.24), kind=kCustom, calls=%fused_computation.7.clone | custom fusion | bytes 1572480 | tf_op jit(solution)/shard_map/jit(_take)/gather | solution.py:39
  300.9 4.3 %reshape.550 = bf16[32,189,64]{1,0,2:T(8,128)(2,1)} reshape(bf16[6048,64]{0,1:T(8,128)(2,1)S(1)} %copy.139) | data formatting | bytes 1548288 | tf_op jit(solution)/shard_map/jit(_take)/gather | solution.py:39
  305.1 18.4 %gather_fusion.18 = bf16[6048,64]{1,0:T(8,128)(2,1)S(1)} fusion(bf16[640,64]{1,0:T(8,128)(2,1)S(1)} %constant_dynamic-update-slice_fusion, s32[6144]{0:T(1024)S(1)} %get-tuple-element.23), kind=kCustom, calls=%fused_computation.8.clone | custom fusion | bytes 1572480 | tf_op jit(solution)/shard_map/jit(_take)/gather | solution.py:39
  328.3 6.0 %fusion.21 = f32[32,8,64]{2,0,1:T(8,128)S(1)} fusion(bf16[189,64,64]{2,1,0:T(8,128)(2,1)} %gather_fusion.5, bf16[32,189,64]{1,0,2:T(8,128)(2,1)} %reshape.514, pred[32,189]{1,0:T(8,128)(4,1)S(1)} %get-tuple-element.50, pred[32,189]{1,0:T(8,128)(4,1)S(1)} %get-tuple-element.58), kind=kOutput, calls=%fused_computation.41 | convolution fusion | flops 50319360 | bytes 2350912 | tf_op jit(solution)/shard_map/dot_general | solution.py:43
  (147 shorter events, 80.5 us)
Async XLA Ops:
  0.0 96.7 %copy-start = (f32[8,64,64]{2,1,0:T(8,128)S(1)}, f32[8,64,64]{2,1,0:T(8,128)}, u32[]{:S(2)}) copy-start(f32[8,64,64]{2,1,0:T(8,128)} %param.32) | copy-start | bytes 393220
  0.0 18.4 %copy-start.15 = (s32[256,189]{0,1:T(8,128)S(1)}, s32[256,189]{0,1:T(8,128)}, u32[]{:S(2)}) copy-start(s32[256,189]{0,1:T(8,128)} %param.25) | copy-start | bytes 580612
  6.0 132.5 %all-to-all-start = ((bf16[8,2,512]{2,1,0:T(2,128)(2,1)}), bf16[8,2,512]{2,1,0:T(2,128)(2,1)S(1)}, u32[]{:S(2)}, u32[]{:S(2)}) async-start(bf16[8,2,512]{2,1,0:T(2,128)(2,1)} %reshape.575), calls=%async_computation | async-start | bytes 32768 | tf_op jit(solution)/shard_map/all_to_all | solution.py:81
  19.0 11.0 %copy-start.14 = (f32[8,64,64]{2,1,0:T(8,128)S(1)}, f32[8,64,64]{2,1,0:T(8,128)}, u32[]{:S(2)}) copy-start(f32[8,64,64]{2,1,0:T(8,128)} %param.31) | copy-start | bytes 393220
  19.0 33.5 %copy-start.16 = (s32[4,189]{1,0:T(4,128)S(1)}, s32[4,189]{1,0:T(4,128)}, u32[]{:S(2)}) copy-start(s32[4,189]{1,0:T(4,128)} %param.28) | copy-start | bytes 9076
  29.1 25.9 %copy-start.17 = (s32[4,189]{1,0:T(4,128)S(1)}, s32[4,189]{1,0:T(4,128)}, u32[]{:S(2)}) copy-start(s32[4,189]{1,0:T(4,128)} %param.29) | copy-start | bytes 9076
  29.1 26.0 %copy-start.22 = (s32[189]{0:T(256)S(1)}, s32[189]{0:T(256)}, u32[]{:S(2)}) copy-start(s32[189]{0:T(256)} %constant.213) | copy-start | bytes 2272
  29.1 26.0 %copy-start.23 = (s32[189]{0:T(256)S(1)}, s32[189]{0:T(256)}, u32[]{:S(2)}) copy-start(s32[189]{0:T(256)} %constant.214) | copy-start | bytes 2272
  29.1 26.0 %copy-start.20 = (s32[189]{0:T(256)S(1)}, s32[189]{0:T(256)}, u32[]{:S(2)}) copy-start(s32[189]{0:T(256)} %constant.215) | copy-start | bytes 2272
  29.1 26.0 %copy-start.21 = (s32[189]{0:T(256)S(1)}, s32[189]{0:T(256)}, u32[]{:S(2)}) copy-start(s32[189]{0:T(256)} %constant.216) | copy-start | bytes 2272
  29.1 26.1 %copy-start.24 = (s32[189]{0:T(256)S(1)}, s32[189]{0:T(256)}, u32[]{:S(2)}) copy-start(s32[189]{0:T(256)} %constant.219) | copy-start | bytes 2272
  83.9 13.0 %copy-start.18 = (s32[189]{0:T(256)S(1)}, s32[189]{0:T(256)}, u32[]{:S(2)}) copy-start(s32[189]{0:T(256)} %constant.217) | copy-start | bytes 2272
  83.9 13.0 %copy-start.19 = (s32[189]{0:T(256)S(1)}, s32[189]{0:T(256)}, u32[]{:S(2)}) copy-start(s32[189]{0:T(256)} %constant.218) | copy-start | bytes 2272
  328.3 6.0 %copy-start.7 = (bf16[189,64,64]{2,1,0:T(8,128)(2,1)S(1)}, bf16[189,64,64]{2,1,0:T(8,128)(2,1)}, u32[]{:S(2)}) copy-start(bf16[189,64,64]{2,1,0:T(8,128)(2,1)} %gather_fusion.7) | copy-start | bytes 4644868
  328.3 6.0 %copy-start.12 = (bf16[32,189,64]{1,0,2:T(8,128)(2,1)S(1)}, bf16[32,189,64]{1,0,2:T(8,128)(2,1)}, u32[]{:S(2)}) copy-start(bf16[32,189,64]{1,0,2:T(8,128)(2,1)} %reshape.520) | copy-start | bytes 2322436
  334.3 3.6 copy-start.6
  334.3 3.6 copy-start.13
  337.9 3.7 %copy-start.5 = (bf16[189,64,64]{2,1,0:T(8,128)(2,1)S(1)}, bf16[189,64,64]{2,1,0:T(8,128)(2,1)}, u32[]{:S(2)}) copy-start(bf16[189,64,64]{2,1,0:T(8,128)(2,1)} %gather_fusion.11) | copy-start | bytes 4644868
  337.9 3.7 %copy-start.10 = (bf16[32,189,64]{1,0,2:T(8,128)(2,1)S(1)}, bf16[32,189,64]{1,0,2:T(8,128)(2,1)}, u32[]{:S(2)}) copy-start(bf16[32,189,64]{1,0,2:T(8,128)(2,1)} %reshape.532) | copy-start | bytes 2322436
  341.7 3.6 copy-start.4
  341.7 3.6 copy-start.11
  348.8 3.6 copy-start.2
  348.8 3.6 copy-start.9
  352.4 3.7 %copy-start.1 = (bf16[189,64,64]{2,1,0:T(8,128)(2,1)S(1)}, bf16[189,64,64]{2,1,0:T(8,128)(2,1)}, u32[]{:S(2)}) copy-start(bf16[189,64,64]{2,1,0:T(8,128)(2,1)} %gather_fusion.19) | copy-start | bytes 4644868
  (2 other events, 7.1 us)
where the time goes:
time: 366 us; the launch traced here: 361 us
  local copies, waits for them, and re-layouts  273 us (75%)
  matrix products  44.8 us (12%)
  blocking collectives  23.9 us (7%)
  other arithmetic  11.2 us (3%)
  starting transfers between devices  7.25 us (2%)
    gather x24, local copies, waits for them, and re-layouts, far_field(): picked = jnp.take(table_rows, grouped_src[:, octant], axis=0)  189 us
    gather x8, local copies, waits for them, and re-layouts, far_field(): jnp.take(m2l_ops, jnp.asarray(vectors[octant]), axis=0).reshape(-1, coeffs)  41.5 us
    dot_general x8, matrix products, far_field(): jnp.dot(picked.reshape(picked.shape[0], -1), flat_ops, preferred_element_...  31.1 us
    all_gather x1, blocking collectives, per_device(): lax.all_gather(coarse_rows, ('leaf', 'sub'), axis=0, tiled=True)  22 us
    gather x1, local copies, waits for them, and re-layouts, per_device(): coarse_ops = jnp.take(m2l_ops, vector_ids, axis=0)  21.5 us
    unnamed x61, local copies, waits for them, and re-layouts  13 us
    dot_general x1, matrix products, per_device(): jnp.einsum('jkc,jkcd->jd', coarse_picked, coarse_ops, preferred_element_t...  12.8 us
  transfers between devices with their start and end apart: 1, of which 0 were waited for; matrix products, arithmetic and copies ran while one was open for 28% of the time, Pallas kernels for 0%

commit v1 on v0

v1 whole, which is shorter than its diff:
```python
import jax
import jax.numpy as jnp
import numpy as np
from jax import lax
from jax.experimental import pallas as pl
from jax.experimental.pallas import tpu as pltpu
from jax.sharding import PartitionSpec as P

LEVELS = 2
LANES = 128
STEP = 8


def list_positions(vec_lanes, dead):
    vector_rank = {}
    for step_x in range(-3, 4):
        for step_y in range(-3, 4):
            for step_z in range(-3, 4):
                if max(abs(step_x), abs(step_y), abs(step_z)) > 1:
                    vector_rank[step_x, step_y, step_z] = len(vector_rank)
    table = np.full((8, vec_lanes), dead, np.int32)
    for octant in range(8):
        shifts = [octant >> position & 1 for position in range(3)]
        entry = 0
        for step_x in range(-2 - shifts[0], 4 - shifts[0]):
            for step_y in range(-2 - shifts[1], 4 - shifts[1]):
                for step_z in range(-2 - shifts[2], 4 - shifts[2]):
                    if max(abs(step_x), abs(step_y), abs(step_z)) > 1:
                        table[octant, vector_rank[step_x, step_y, step_z]] = entry
                        entry += 1
    return table


def round_up(value, unit):
    return -(-value // unit) * unit


def gather_lanes(values, index):
    return jnp.take_along_axis(values, index, axis=1, mode="promise_in_bounds")


def spread_lists(rows, positions):
    pieces = []
    for out in range(positions.shape[1] // LANES):
        where = positions[:, out * LANES : (out + 1) * LANES]
        low = where & (LANES - 1)
        high = where >> 7
        value = gather_lanes(rows[:, :LANES], low)
        for seg in range(1, rows.shape[1] // LANES):
            other = gather_lanes(rows[:, seg * LANES : (seg + 1) * LANES], low)
            value = jnp.where(high == seg, other, value)
        pieces.append(value)
    return pieces


def leaf_kernel(idx_ref, pos_ref, table_ref, ops_ref, out_ref, low_ref, high_ref, acc_ref):
    steps, coeffs, _ = ops_ref.shape
    targets = idx_ref.shape[1]
    width = table_ref.shape[1]
    segs = table_ref.shape[0] // coeffs
    rows = jnp.transpose(idx_ref[...])
    where = jnp.concatenate([pos_ref[...]] * (targets // 8), axis=0)
    for out, piece in enumerate(spread_lists(rows, where)):
        block = jnp.transpose(piece)
        low_ref[out * LANES : (out + 1) * LANES, :] = (block % width).astype(jnp.float32)
        high_ref[out * LANES : (out + 1) * LANES, :] = block // width
    acc_ref[...] = jnp.zeros_like(acc_ref)
    ladder = lax.broadcasted_iota(jnp.int32, (width, LANES), 0).astype(jnp.float32)
    ladder = ladder.astype(jnp.bfloat16)
    one = jnp.ones((), jnp.bfloat16)
    nothing = jnp.zeros((), jnp.bfloat16)

    def step(at, carry):
        base = pl.multiple_of(at * STEP, STEP)
        lows = low_ref[pl.ds(base, STEP), :]
        highs = high_ref[pl.ds(base, STEP), :]
        picked = []
        for vec in range(STEP):
            columns = []
            for tile in range(targets // LANES):
                low = lows[vec : vec + 1, tile * LANES : (tile + 1) * LANES]
                low = jnp.broadcast_to(low, (16, LANES)).astype(jnp.bfloat16)
                low = jnp.concatenate([low] * (width // 16), axis=0)
                columns.append(jnp.where(low == ladder, one, nothing))
            chosen = jnp.concatenate(columns, axis=1)
            found = jnp.dot(table_ref[...], chosen, preferred_element_type=jnp.float32)
            high = jnp.broadcast_to(highs[vec : vec + 1, :], (coeffs, targets))
            value = jnp.zeros((coeffs, targets), jnp.float32)
            for seg in range(segs):
                value = jnp.where(high == seg, found[seg * coeffs : (seg + 1) * coeffs], value)
            picked.append(value.astype(jnp.bfloat16))
        acc_ref[...] += jnp.dot(
            ops_ref[at], jnp.concatenate(picked, axis=0), preferred_element_type=jnp.float32
        )
        return carry

    lax.fori_loop(0, steps, step, 0)
    out_ref[...] = acc_ref[...]


def leaf_far(idx, positions, table, ops):
    coeffs = ops.shape[1]
    targets = idx.shape[1]
    vec_lanes = positions.shape[1]
    return pl.pallas_call(
        leaf_kernel,
        out_shape=jax.ShapeDtypeStruct((coeffs, targets), jnp.float32),
        in_specs=[pl.BlockSpec(memory_space=pltpu.VMEM)] * 4,
        out_specs=pl.BlockSpec(memory_space=pltpu.VMEM),
        scratch_shapes=[
            pltpu.VMEM((vec_lanes, targets), jnp.float32),
            pltpu.VMEM((vec_lanes, targets), jnp.int32),
            pltpu.VMEM((coeffs, targets), jnp.float32),
        ],
        compiler_params=pltpu.CompilerParams(vmem_limit_bytes=40 * 1024 * 1024),
        cost_estimate=pl.CostEstimate(
            flops=20_000_000_000, bytes_accessed=4_000_000, transcendentals=0
        ),
        name="leaf_far",
    )(idx, positions, table, ops)


def coarse_kernel(idx_ref, pos_ref, table_ref, ops_ref, out_ref):
    coeffs, _, vecs = ops_ref.shape
    pieces = spread_lists(idx_ref[...], pos_ref[...])
    lows = [piece & (LANES - 1) for piece in pieces]
    highs = [piece >> 7 for piece in pieces]
    segs = table_ref.shape[1] // LANES

    def step(at, total):
        base = pl.multiple_of(at * STEP, STEP)
        block = table_ref[pl.ds(base, STEP), :]
        for coeff in range(STEP):
            columns = []
            for low, high in zip(lows, highs):
                value = jnp.zeros(low.shape, jnp.float32)
                for seg in range(segs):
                    row = block[coeff : coeff + 1, seg * LANES : (seg + 1) * LANES]
                    other = gather_lanes(jnp.broadcast_to(row, low.shape), low)
                    value = jnp.where(high == seg, other, value)
                columns.append(value)
            picked = jnp.concatenate(columns, axis=1)[:, :vecs].astype(jnp.bfloat16)
            total += lax.dot_general(
                picked,
                ops_ref[base + coeff],
                (((1,), (1,)), ((), ())),
                preferred_element_type=jnp.float32,
            )
        return total

    out_ref[...] = lax.fori_loop(
        0, coeffs // STEP, step, jnp.zeros(out_ref.shape, jnp.float32)
    )


def coarse_far(idx, positions, table, ops):
    return pl.pallas_call(
        coarse_kernel,
        out_shape=jax.ShapeDtypeStruct((idx.shape[0], ops.shape[0]), jnp.float32),
        in_specs=[pl.BlockSpec(memory_space=pltpu.VMEM)] * 4,
        out_specs=pl.BlockSpec(memory_space=pltpu.VMEM),
        compiler_params=pltpu.CompilerParams(vmem_limit_bytes=40 * 1024 * 1024),
        cost_estimate=pl.CostEstimate(
            flops=2_000_000_000, bytes_accessed=4_000_000, transcendentals=0
        ),
        name="coarse_far",
    )(idx, positions, table, ops)


def upward(children, m2m_ops):
    grouped = children.reshape(-1, 8, children.shape[-1])
    return jnp.einsum("noc,ocd->nd", grouped, m2m_ops, precision=lax.Precision.HIGHEST)


def downward(parents, l2l_ops):
    spread = jnp.einsum("nc,ocd->nod", parents, l2l_ops, precision=lax.Precision.HIGHEST)
    return spread.reshape(-1, parents.shape[-1])


def per_device(
    multipoles,
    list_src,
    list_mask,
    send_boxes,
    send_count,
    coarse_src,
    coarse_mask,
    m2l_ops,
    m2m_ops,
    l2l_ops,
):
    boxes, coeffs = multipoles.shape
    entries = list_src.shape[1]
    vecs = m2l_ops.shape[0]
    count_leaf = lax.axis_size("leaf")
    count_sub = lax.axis_size("sub")
    capacity = send_boxes.shape[2]
    bits = count_leaf.bit_length() - 1
    me = lax.axis_index("leaf")
    chip = boxes * count_sub
    segs = count_sub + -(-bits * capacity // boxes)
    by_coeff = multipoles.T

    current = multipoles.astype(jnp.float32)
    for level_step in range(LEVELS):
        current = upward(current, m2m_ops)
    coarse_rows = current.astype(jnp.bfloat16)
    all_coarse = lax.all_gather(coarse_rows, ("leaf", "sub"), axis=0, tiled=True)

    chip_part = lax.all_gather(by_coeff, "sub", axis=0, tiled=True)
    peers = jnp.bitwise_xor(me, jnp.left_shift(1, jnp.arange(bits, dtype=jnp.int32)))
    is_peer = peers[:, None] == jnp.arange(count_leaf, dtype=jnp.int32)[None, :]
    wanted = jnp.sum(jnp.where(is_peer[:, :, None], send_boxes[0][None], 0), axis=1)
    limit = jnp.sum(jnp.where(is_peer, send_count[0][None], 0), axis=1)
    live = jnp.arange(capacity, dtype=jnp.int32)[None, :] < limit[:, None]
    wanted = jnp.where(live, wanted, -1).reshape(1, -1)
    chosen = (jnp.arange(boxes, dtype=jnp.int32)[:, None] == wanted).astype(multipoles.dtype)
    outgoing = jnp.dot(by_coeff, chosen, preferred_element_type=multipoles.dtype)
    incoming = []
    for bit in range(bits):
        pairs = [(leaf, leaf ^ (1 << bit)) for leaf in range(count_leaf)]
        part = outgoing[:, bit * capacity : (bit + 1) * capacity]
        incoming.append(lax.ppermute(part, "leaf", pairs))
    far_width = (segs - count_sub) * boxes
    incoming = jnp.concatenate(incoming, axis=1)
    incoming = jnp.pad(incoming, ((0, 0), (0, far_width - bits * capacity)))
    incoming = incoming.reshape(coeffs, -1, boxes).transpose(1, 0, 2).reshape(-1, boxes)
    table = jnp.concatenate([chip_part, incoming], axis=0)

    entry_lanes = round_up(entries + 1, LANES)
    vec_lanes = round_up(vecs, LANES)
    positions = list_positions(vec_lanes, entry_lanes - 1)
    source = list_src.T
    remote = source - chip
    distance = jnp.bitwise_xor(remote // capacity, me)
    which = jnp.zeros_like(distance)
    for bit in range(1, bits):
        which += (distance >= (1 << bit)).astype(jnp.int32)
    row = jnp.where(source < chip, source, chip + which * capacity + remote % capacity)
    row = jnp.where(list_mask.T > 0, row, segs * boxes)
    row = jnp.pad(
        row, ((0, entry_lanes - entries), (0, 0)), constant_values=segs * boxes
    )
    steps = -(-vecs // STEP)
    ops = jnp.pad(m2l_ops, ((0, steps * STEP - vecs), (0, 0), (0, 0)))
    ops = ops.reshape(steps, STEP, coeffs, coeffs).transpose(0, 3, 1, 2)
    ops = ops.reshape(steps, coeffs, STEP * coeffs)
    far_leaf = leaf_far(row, jnp.asarray(positions), table, ops)

    count_coarse = coarse_rows.shape[0]
    height = round_up(count_coarse, 8)
    dead = all_coarse.shape[0]
    coarse_lanes = round_up(dead + 1, LANES)
    coarse_table = jnp.pad(
        all_coarse.T.astype(jnp.float32), ((0, 0), (0, coarse_lanes - dead))
    )
    coarse_row = jnp.where(coarse_mask > 0, coarse_src, dead)
    coarse_row = jnp.pad(
        coarse_row,
        ((0, height - count_coarse), (0, entry_lanes - entries)),
        constant_values=dead,
    )
    first_coarse = lax.axis_index(("leaf", "sub")) * count_coarse
    doubled = jnp.asarray(np.concatenate([positions, positions], axis=0))
    coarse_positions = lax.dynamic_slice_in_dim(doubled, first_coarse % 8, height, 0)
    inherited = coarse_far(
        coarse_row, coarse_positions, coarse_table, m2l_ops.transpose(1, 2, 0)
    )[:count_coarse]
    for level_step in range(LEVELS):
        inherited = downward(inherited, l2l_ops)
    return far_leaf.T + inherited


def solution(mesh):
    placed = (
        P(("groups", "leaf", "sub"), None),
        P(("groups", "leaf", "sub"), None),
        P(("groups", "leaf", "sub"), None),
        P(("groups", "leaf", "sub"), None, None),
        P(("groups", "leaf", "sub"), None),
        P(("groups", "leaf", "sub"), None),
        P(("groups", "leaf", "sub"), None),
        P(),
        P(),
        P(),
    )
    return jax.shard_map(
        per_device,
        mesh=mesh,
        in_specs=placed,
        out_specs=P(("groups", "leaf", "sub"), None),
        check_vma=False,
    )
```

time: 366 us -> 85.4 us (0.23); the launches traced: 361 us -> 84.7 us
  local copies, waits for them, and re-layouts: 273 us -> 24.8 us
  matrix products: 44.8 us -> 3.85 us
  Pallas kernels: 0 us -> 24.3 us
  other arithmetic: 11.2 us -> 4.9 us
  blocking collectives: 23.9 us -> 19.6 us
    gather x38 -> x0, local copies, waits for them, and re-layouts: 257 us -> none  [the longest x24 189 us: far_field(): picked = jnp.take(table_rows, grouped_src[:, octant], axis=0)]
    dot_general x9 -> x1, matrix products: 43.8 us -> 0.91 us  [per_device(): jnp.dot(by_coeff, chosen, preferred_element_type=multipoles.dtype)]
    pallas_call x0 -> x2, Pallas kernels: none -> 24.3 us  [the longest x1 21.7 us: leaf_far(): pl.pallas_call(leaf_kernel, out_shape=jax.ShapeDtypeStruct((coeffs, targe...]
    all_to_all x1 -> x0, starting transfers between devices: 7.25 us -> none  [per_device(): lax.all_to_all(outgoing, 'leaf', split_axis=0, concat_axis=0, tiled=True)]
    select_n x16 -> x3, other arithmetic: 8.86 us -> 1.73 us  [the longest x1 0.95 us: per_device(): row = jnp.where(list_mask.T > 0, row, segs * boxes)]
    ppermute x0 -> x3, starting transfers between devices: none -> 7.1 us  [per_device(): incoming.append(lax.ppermute(part, 'leaf', pairs))]
    pad x0 -> x3, local copies, waits for them, and re-layouts: none -> 6.2 us  [the longest x1 6.17 us: per_device(): ops = jnp.pad(m2l_ops, ((0, steps * STEP - vecs), (0, 0), (0, 0)))]
    reshape x1 -> x2, local copies, waits for them, and re-layouts: 0.1 us -> 4.81 us  [the longest x1 4.73 us: per_device(): ops = ops.reshape(steps, coeffs, STEP * coeffs)]
  transfers between devices with their start and end apart: 1 -> 3, of which waited for: 0 -> 0; matrix products, arithmetic and copies ran while one was open for 28% -> 32% of each run, Pallas kernels for 0% -> 3%
where the time goes in v1:
time: 85.4 us; the launch traced here: 84.7 us
  local copies, waits for them, and re-layouts  24.8 us (29%)
  Pallas kernels  24.3 us (28%)
  blocking collectives  19.6 us (23%)
  starting transfers between devices  7.1 us (8%)
  other arithmetic  4.9 us (6%)
  matrix products  3.85 us (5%)
    pallas_call x1, Pallas kernels, leaf_far(): pl.pallas_call(leaf_kernel, out_shape=jax.ShapeDtypeStruct((coeffs, targe...  21.7 us
    all_gather x1, blocking collectives, per_device(): lax.all_gather(coarse_rows, ('leaf', 'sub'), axis=0, tiled=True)  17.6 us
    unnamed x21, local copies, waits for them, and re-layouts  12.2 us
    ppermute x3, starting transfers between devices, per_device(): incoming.append(lax.ppermute(part, 'leaf', pairs))  7.1 us
    pad x1, local copies, waits for them, and re-layouts, per_device(): ops = jnp.pad(m2l_ops, ((0, steps * STEP - vecs), (0, 0), (0, 0)))  6.17 us
    reshape x1, local copies, waits for them, and re-layouts, per_device(): ops = ops.reshape(steps, coeffs, STEP * coeffs)  4.73 us
    pallas_call x1, Pallas kernels, coarse_far(): pl.pallas_call(coarse_kernel, out_shape=jax.ShapeDtypeStruct((idx.shape[0...  2.55 us
    dot_general x2, matrix products, upward(): jnp.einsum('noc,ocd->nd', grouped, m2m_ops, precision=lax.Precision.HIGHEST)  2.41 us
  transfers between devices with their start and end apart: 3, of which 0 were waited for; matrix products, arithmetic and copies ran while one was open for 32% of the time, Pallas kernels for 3%

profile of v1, /device:TPU:0, one launch (start us, length us, event | category | flops | bytes accessed | tf_op | source)
XLA Modules:
  0.0 84.7 jit_solution(6641917763747843099)
XLA Ops:
  0.1 0.8 select_reduce_fusion.1
  0.9 0.8 select_reduce_fusion
  1.9 0.9 %convolution_bitcast_fusion.1 = bf16[64,48]{1,0:T(8,128)(2,1)S(1)} fusion(bf16[256,64]{0,1:T(8,128)(2,1)} %param.12, s32[48]{0:T(128)S(1)} %select_n.58), kind=kOutput, calls=%fused_computation.1 | convolution fusion | flops 1585152 | bytes 39104 | tf_op jit(solution)/shard_map/dot_general | solution.py:218
  2.8 0.7 fusion.22
  3.4 2.9 %collective-permute-start = (bf16[64,16]{1,0:T(8,128)(2,1)}, bf16[64,16]{1,0:T(8,128)(2,1)S(1)}, u32[]{:S(2)}, u32[]{:S(2)}) collective-permute-start(bf16[64,16]{1,0:T(8,128)(2,1)} %get-tuple-element.5), channel_id=1, source_target_pairs={{0,2},{2,0},{4,6},{6,4},{8,10},{10,8},{12,14},{14,12},{1,3},{3,1},... | collective-permute-start | bytes 6152 | tf_op jit(solution)/shard_map/ppermute | solution.py:223
  6.4 2.6 %collective-permute-start.2 = (bf16[64,16]{1,0:T(8,128)(2,1)}, bf16[64,16]{1,0:T(8,128)(2,1)}, u32[]{:S(2)}, u32[]{:S(2)}) collective-permute-start(bf16[64,16]{1,0:T(8,128)(2,1)} %get-tuple-element.6), channel_id=1, source_target_pairs={{0,8},{2,10},{4,12},{6,14},{8,0},{10,2},{12,4},{14,6},{1,9},{3,11}... | collective-permute-start | bytes 6152 | tf_op jit(solution)/shard_map/ppermute | solution.py:223
  9.0 1.6 %collective-permute-start.1 = (bf16[64,16]{1,0:T(8,128)(2,1)}, bf16[64,16]{1,0:T(8,128)(2,1)}, u32[]{:S(2)}, u32[]{:S(2)}) collective-permute-start(bf16[64,16]{1,0:T(8,128)(2,1)} %get-tuple-element.7), channel_id=1, source_target_pairs={{0,4},{2,6},{4,0},{6,2},{8,12},{10,14},{12,8},{14,10},{1,5},{3,7},... | collective-permute-start | bytes 6152 | tf_op jit(solution)/shard_map/ppermute | solution.py:223
  10.6 0.9 %copy.38 = bf16[256,64]{1,0:T(8,128)(2,1)S(1)} copy(bf16[256,64]{0,1:T(8,128)(2,1)} %param.12) | data formatting | bytes 65536 | tf_op args[0]
  11.4 1.2 %convolution_bitcast_fusion = f32[4,8,64]{2,1,0:T(8,128)S(1)} fusion(f32[8,64,64]{2,1,0:T(8,128)} %param.20, bf16[4,8,64,8]{2,3,1,0:T(8,128)(2,1)S(1)} %bitcast.59), kind=kOutput, calls=%fused_computation | convolution fusion | flops 12582912 | bytes 172032 | tf_op jit(solution)/shard_map/noc,ocd->nd/dot_general | solution.py:172
  12.6 1.2 %fusion.1 = bf16[1,4,64]{2,1,0:T(4,128)(2,1)S(1)} fusion(f32[8,64,64]{2,1,0:T(8,128)} %param.20, f32[4,8,64]{2,1,0:T(8,128)S(1)} %convolution_bitcast_fusion), kind=kOutput, calls=%fused_computation.4 | convolution fusion | flops 1573120 | bytes 139776 | tf_op jit(solution)/shard_map/noc,ocd->nd/dot_general | solution.py:172
  13.9 17.6 %all-gather = bf16[16,4,64]{2,1,0:T(4,128)(2,1)S(1)} all-gather(bf16[1,4,64]{2,1,0:T(4,128)(2,1)S(1)} %fusion.1), channel_id=1, replica_groups=mesh['groups'=2,'leaf'=8,'sub'=2] {'leaf','sub'}, dimensions={0}, use_global_device_ids=true | all-gather | bytes 8704 | tf_op jit(solution)/shard_map/all_gather | solution.py:208
  31.6 0.7 compare_select_fusion.1
  32.3 0.7 constant_dynamic-slice_fusion.pos_ref
  33.1 1.9 %copy-done.1 = bf16[316,64,64]{0,2,1:T(8,128)(2,1)S(1)} copy-done((bf16[316,64,64]{0,2,1:T(8,128)(2,1)S(1)}, bf16[316,64,64]{0,2,1:T(8,128)(2,1)}, u32[]{:S(2)}) %copy-start.1) | copy-done | bytes 2588696
  35.0 2.5 %coarse_far.1 = f32[8,64]{1,0:T(8,128)S(1)} custom-call(s32[8,256]{1,0:T(8,128)S(1)} %pad.25.idx_ref, s32[8,384]{1,0:T(8,128)S(1)} %constant_dynamic-slice_fusion.pos_ref, f32[64,128]{1,0:T(8,128)S(1)} %pad_convert_fusion.table_ref, bf16[64,64,316]{2,1,0:T(8,128)(2,1)S(1)} %bitcast.56), custom_call_target="tpu_custom_call" | custom-call | flops 2000000000 | bytes 4000000 | tf_op jit(solution)/shard_map/coarse_far/pallas_call | solution.py:157
  37.8 0.3 fusion.14
  38.1 0.9 %fusion.5 = s32[189,256]{1,0:T(8,128)} fusion(s32[256,189]{0,1:T(8,128)S(1)} %copy-done.6, s32[256,189]{0,1:T(8,128)S(1)} %copy-done.7, s32[]{:T(128)S(6)} %axis_index.27), kind=kLoop, calls=%fused_computation.14 | loop fusion | flops 1596672 | bytes 580612 | tf_op jit(solution)/shard_map/jit(_where)/select_n | solution.py:240
  39.0 2.0 %all_gather.6 = bf16[128,256]{1,0:T(8,128)(2,1)} all-gather(bf16[64,256]{1,0:T(8,128)(2,1)S(1)} %bitcast.60), channel_id=1, replica_groups=mesh['groups'=2,'leaf'=8,'sub'=2] {'sub'}, dimensions={0}, use_global_device_ids=true | all-gather | bytes 98304 | tf_op jit(solution)/shard_map/all_gather | solution.py:210
  41.0 9.3 %copy.36 = bf16[316,64,64]{2,1,0:T(8,128)(2,1)} copy(bf16[316,64,64]{0,2,1:T(8,128)(2,1)S(1)} %copy-done.2) | data formatting | bytes 5177344 | tf_op args[7]
  50.5 6.2 %pad.24 = bf16[320,64,64]{2,1,0:T(8,128)(2,1)} pad(bf16[316,64,64]{2,1,0:T(8,128)(2,1)} %copy.36, bf16[]{:T(256)} %constant.71.clone.1), padding=0_4x0_0x0_0 | pad | bytes 5210114 | tf_op jit(solution)/shard_map/jit(_pad)/pad | solution.py:245
  56.6 4.7 %copy.47.ops_ref = bf16[40,64,512]{2,1,0:T(8,128)(2,1)S(1)} copy(bf16[40,64,512]{1,2,0:T(8,128)(2,1)} %bitcast.57) | data formatting | bytes 5242880 | tf_op jit(solution)/shard_map/reshape | solution.py:247
  61.5 0.8 fusion.13
  62.3 21.7 %leaf_far.1 = f32[64,256]{1,0:T(8,128)S(1)} custom-call(s32[256,256]{1,0:T(8,128)S(1)} %pad.22.idx_ref, s32[8,384]{1,0:T(8,128)S(1)} %copy-done.3, bf16[192,256]{1,0:T(8,128)(2,1)S(1)} %pad_maximum_fusion.table_ref, bf16[40,64,512]{2,1,0:T(8,128)(2,1)S(1)} %copy.47.ops_ref), custom_call_target="tpu_custom_call" | custom-call | flops 20000000000 | bytes 4000000 | tf_op jit(solution)/shard_map/leaf_far/pallas_call | solution.py:105
  84.1 0.6 bitcast_add_fusion.1
  (32 shorter events, 0.8 us)
Async XLA Ops:
  0.0 37.5 %copy-start = (f32[8,64,64]{2,1,0:T(8,128)S(1)}, f32[8,64,64]{2,1,0:T(8,128)}, u32[]{:S(2)}) copy-start(f32[8,64,64]{2,1,0:T(8,128)} %param.21) | copy-start | bytes 393220
  3.4 58.0 %collective-permute-start = (bf16[64,16]{1,0:T(8,128)(2,1)}, bf16[64,16]{1,0:T(8,128)(2,1)S(1)}, u32[]{:S(2)}, u32[]{:S(2)}) collective-permute-start(bf16[64,16]{1,0:T(8,128)(2,1)} %get-tuple-element.5), channel_id=1, source_target_pairs={{0,2},{2,0},{4,6},{6,4},{8,10},{10,8},{12,14},{14,12},{1,3},{3,1},... | collective-permute-start | bytes 6152 | tf_op jit(solution)/shard_map/ppermute | solution.py:223
  6.4 55.0 %collective-permute-start.2 = (bf16[64,16]{1,0:T(8,128)(2,1)}, bf16[64,16]{1,0:T(8,128)(2,1)}, u32[]{:S(2)}, u32[]{:S(2)}) collective-permute-start(bf16[64,16]{1,0:T(8,128)(2,1)} %get-tuple-element.6), channel_id=1, source_target_pairs={{0,8},{2,10},{4,12},{6,14},{8,0},{10,2},{12,4},{14,6},{1,9},{3,11}... | collective-permute-start | bytes 6152 | tf_op jit(solution)/shard_map/ppermute | solution.py:223
  9.0 52.5 %collective-permute-start.1 = (bf16[64,16]{1,0:T(8,128)(2,1)}, bf16[64,16]{1,0:T(8,128)(2,1)}, u32[]{:S(2)}, u32[]{:S(2)}) collective-permute-start(bf16[64,16]{1,0:T(8,128)(2,1)} %get-tuple-element.7), channel_id=1, source_target_pairs={{0,4},{2,6},{4,0},{6,2},{8,12},{10,14},{12,8},{14,10},{1,5},{3,7},... | collective-permute-start | bytes 6152 | tf_op jit(solution)/shard_map/ppermute | solution.py:223
  31.6 7.4 %copy-start.8 = (bf16[256,64]{0,1:T(8,128)(2,1)S(1)}, bf16[256,64]{0,1:T(8,128)(2,1)}, u32[]{:S(2)}) copy-start(bf16[256,64]{0,1:T(8,128)(2,1)} %param.12) | copy-start | bytes 98308
  33.1 1.9 %copy-start.1 = (bf16[316,64,64]{0,2,1:T(8,128)(2,1)S(1)}, bf16[316,64,64]{0,2,1:T(8,128)(2,1)}, u32[]{:S(2)}) copy-start(bf16[316,64,64]{0,2,1:T(8,128)(2,1)} %param.19) | copy-start | bytes 7766020
  35.0 3.1 %copy-start.6 = (s32[256,189]{0,1:T(8,128)S(1)}, s32[256,189]{0,1:T(8,128)}, u32[]{:S(2)}) copy-start(s32[256,189]{0,1:T(8,128)} %param.13) | copy-start | bytes 580612
  35.0 3.1 %copy-start.7 = (s32[256,189]{0,1:T(8,128)S(1)}, s32[256,189]{0,1:T(8,128)}, u32[]{:S(2)}) copy-start(s32[256,189]{0,1:T(8,128)} %param.14) | copy-start | bytes 580612
  35.0 6.0 %copy-start.2 = (bf16[316,64,64]{0,2,1:T(8,128)(2,1)S(1)}, bf16[316,64,64]{0,2,1:T(8,128)(2,1)}, u32[]{:S(2)}) copy-start(bf16[316,64,64]{0,2,1:T(8,128)(2,1)} %param.19) | copy-start | bytes 7766020
  56.6 4.7 %copy-start.4 = (s32[189,256]{1,0:T(8,128)S(1)}, s32[189,256]{1,0:T(8,128)}, u32[]{:S(2)}) copy-start(s32[189,256]{1,0:T(8,128)} %fusion.5) | copy-start | bytes 580612
  56.6 5.6 %copy-start.5 = (bf16[128,256]{1,0:T(8,128)(2,1)S(1)}, bf16[128,256]{1,0:T(8,128)(2,1)}, u32[]{:S(2)}) copy-start(bf16[128,256]{1,0:T(8,128)(2,1)} %all_gather.6) | copy-start | bytes 196612
  56.6 5.7 %copy-start.3 = (s32[8,384]{1,0:T(8,128)S(1)}, s32[8,384]{1,0:T(8,128)}, u32[]{:S(2)}) copy-start(s32[8,384]{1,0:T(8,128)} %constant.75.clone.pos_ref) | copy-start | bytes 36868

commit v2 on v1

v2 whole, which is shorter than its diff:
```python
import jax
import jax.numpy as jnp
import numpy as np
from jax import lax
from jax.experimental import pallas as pl
from jax.experimental.pallas import tpu as pltpu
from jax.sharding import PartitionSpec as P

LEVELS = 2
LANES = 128
STEP = 8


def list_positions(vec_lanes, dead):
    vector_rank = {}
    for step_x in range(-3, 4):
        for step_y in range(-3, 4):
            for step_z in range(-3, 4):
                if max(abs(step_x), abs(step_y), abs(step_z)) > 1:
                    vector_rank[step_x, step_y, step_z] = len(vector_rank)
    table = np.full((8, vec_lanes), dead, np.int32)
    for octant in range(8):
        shifts = [octant >> position & 1 for position in range(3)]
        entry = 0
        for step_x in range(-2 - shifts[0], 4 - shifts[0]):
            for step_y in range(-2 - shifts[1], 4 - shifts[1]):
                for step_z in range(-2 - shifts[2], 4 - shifts[2]):
                    if max(abs(step_x), abs(step_y), abs(step_z)) > 1:
                        table[octant, vector_rank[step_x, step_y, step_z]] = entry
                        entry += 1
    return table


def round_up(value, unit):
    return -(-value // unit) * unit


def gather_lanes(values, index):
    return jnp.take_along_axis(values, index, axis=1, mode="promise_in_bounds")


def spread_lists(rows, positions):
    pieces = []
    for out in range(positions.shape[1] // LANES):
        where = positions[:, out * LANES : (out + 1) * LANES]
        low = where & (LANES - 1)
        high = where >> 7
        value = gather_lanes(rows[:, :LANES], low)
        for seg in range(1, rows.shape[1] // LANES):
            other = gather_lanes(rows[:, seg * LANES : (seg + 1) * LANES], low)
            value = jnp.where(high == seg, other, value)
        pieces.append(value)
    return pieces


def exchange_kernel(
    mine_ref, boxes_ref, counts_ref, coarse_ref, table_ref, all_coarse_ref,
    outbox, inbox, chip_sems, box_sems, send_sems, recv_sems,
):
    coeffs, boxes = mine_ref.shape
    count_leaf, capacity = boxes_ref.shape
    bits = inbox.shape[0]
    lanes = outbox.shape[1]
    members = all_coarse_ref.shape[0]
    count_sub = members // count_leaf
    leaf = lax.axis_index("leaf")
    sub = lax.axis_index("sub")
    me = leaf * count_sub + sub

    def place(other):
        return {"leaf": other // count_sub, "sub": other % count_sub}

    barrier = pltpu.get_barrier_semaphore()

    def greet(step, carry):
        pl.semaphore_signal(barrier, inc=1, device_id=place(jnp.bitwise_xor(me, step)))
        return carry

    lax.fori_loop(1, members, greet, 0)

    slots = lax.broadcasted_iota(jnp.int32, (1, capacity), 1)
    leaves = lax.broadcasted_iota(jnp.int32, (1, count_leaf), 1)
    wanted = []
    for bit in range(bits):
        peer = jnp.bitwise_xor(leaf, 1 << bit)
        limit = jnp.sum(
            jnp.where(leaves == peer, counts_ref[...], 0), axis=1, keepdims=True
        )
        wanted.append(jnp.where(slots < limit, boxes_ref[pl.ds(peer, 1), :], -1))
    wanted.append(jnp.full((1, lanes - bits * capacity), -1, jnp.int32))
    wanted = jnp.broadcast_to(jnp.concatenate(wanted, axis=1), (boxes, lanes))
    ladder = lax.broadcasted_iota(jnp.int32, (boxes, lanes), 0)
    chosen = jnp.where(wanted == ladder, 1.0, 0.0).astype(jnp.bfloat16)
    outbox[...] = jnp.dot(
        mine_ref[...], chosen, preferred_element_type=jnp.float32
    ).astype(jnp.bfloat16)

    pl.semaphore_wait(barrier, members - 1)
    own = pl.ds(pl.multiple_of(sub * coeffs, coeffs), coeffs)
    chip_copy = pltpu.make_async_remote_copy(
        src_ref=mine_ref,
        dst_ref=table_ref.at[own],
        send_sem=chip_sems.at[0],
        recv_sem=chip_sems.at[1],
        device_id={"sub": 1 - sub},
    )
    chip_copy.start()
    box_copies = []
    for bit in range(bits):
        copy = pltpu.make_async_remote_copy(
            src_ref=outbox,
            dst_ref=inbox.at[bit],
            send_sem=box_sems.at[0, bit],
            recv_sem=box_sems.at[1, bit],
            device_id={"leaf": jnp.bitwise_xor(leaf, 1 << bit)},
        )
        copy.start()
        box_copies.append(copy)

    def coarse_copy(step):
        return pltpu.make_async_remote_copy(
            src_ref=coarse_ref,
            dst_ref=all_coarse_ref.at[me],
            send_sem=send_sems.at[step],
            recv_sem=recv_sems.at[step],
            device_id=place(jnp.bitwise_xor(me, step)),
        )

    def send(step, carry):
        coarse_copy(step).start()
        return carry

    def finish(step, carry):
        coarse_copy(step).wait()
        return carry

    lax.fori_loop(1, members, send, 0)
    all_coarse_ref[pl.ds(me, 1)] = coarse_ref[...][None]
    table_ref[own, :] = mine_ref[...]
    for copy in box_copies:
        copy.wait()
    column = lax.broadcasted_iota(jnp.int32, (coeffs, lanes), 1) // capacity
    far = jnp.zeros((coeffs, lanes), jnp.float32)
    for bit in range(bits):
        far = jnp.where(column == bit, inbox[bit].astype(jnp.float32), far)
    table_ref[count_sub * coeffs :, :lanes] = far.astype(jnp.bfloat16)
    table_ref[count_sub * coeffs :, lanes:] = jnp.zeros(
        (coeffs, boxes - lanes), jnp.bfloat16
    )
    chip_copy.wait()
    lax.fori_loop(1, members, finish, 0)


def exchange(mine, send_boxes, send_count, coarse, members, bits):
    coeffs, boxes = mine.shape
    lanes = round_up(bits * send_boxes.shape[1], LANES)
    return pl.pallas_call(
        exchange_kernel,
        out_shape=(
            jax.ShapeDtypeStruct((3 * coeffs, boxes), jnp.bfloat16),
            jax.ShapeDtypeStruct((members,) + coarse.shape, jnp.float32),
        ),
        in_specs=[pl.BlockSpec(memory_space=pltpu.VMEM)] * 4,
        out_specs=[pl.BlockSpec(memory_space=pltpu.VMEM)] * 2,
        scratch_shapes=[
            pltpu.VMEM((coeffs, lanes), jnp.bfloat16),
            pltpu.VMEM((bits, coeffs, lanes), jnp.bfloat16),
            pltpu.SemaphoreType.DMA((2,)),
            pltpu.SemaphoreType.DMA((2, bits)),
            pltpu.SemaphoreType.DMA((members,)),
            pltpu.SemaphoreType.DMA((members,)),
        ],
        compiler_params=pltpu.CompilerParams(
            collective_id=0, has_side_effects=True, vmem_limit_bytes=24 * 1024 * 1024
        ),
        name="exchange",
    )(mine, send_boxes, send_count, coarse)


def leaf_kernel(
    idx_ref, pos_ref, table_ref, coarse_idx_ref, coarse_pos_ref, coarse_ref, ops_ref,
    out_ref, coarse_out_ref, low_ref, high_ref, picks_ref, acc_ref, coarse_table_ref,
):
    coeffs, _, vecs = ops_ref.shape
    targets = idx_ref.shape[1]
    width = table_ref.shape[1]
    segs = table_ref.shape[0] // coeffs
    vec_rows = picks_ref.shape[1] // coeffs
    tiles = targets // LANES
    rows = jnp.transpose(idx_ref[...])
    where = jnp.concatenate([pos_ref[...]] * (targets // 8), axis=0)
    for out, piece in enumerate(spread_lists(rows, where)):
        block = jnp.transpose(piece)
        low_ref[out * LANES : (out + 1) * LANES, :] = (block % width).astype(jnp.float32)
        high_ref[out * LANES : (out + 1) * LANES, :] = block // width
    acc_ref[...] = jnp.zeros_like(acc_ref)
    ladder = lax.broadcasted_iota(jnp.int32, (width, LANES), 0).astype(jnp.float32)
    ladder = ladder.astype(jnp.bfloat16)
    one = jnp.ones((), jnp.bfloat16)
    nothing = jnp.zeros((), jnp.bfloat16)

    def pick(at, carry):
        base = pl.multiple_of(at * STEP, STEP)
        lows = low_ref[pl.ds(base, STEP), :]
        highs = high_ref[pl.ds(base, STEP), :]
        for vec in range(STEP):
            columns = []
            for tile in range(tiles):
                low = lows[vec : vec + 1, tile * LANES : (tile + 1) * LANES]
                low = jnp.broadcast_to(low, (16, LANES)).astype(jnp.bfloat16)
                low = jnp.concatenate([low] * (width // 16), axis=0)
                columns.append(jnp.where(low == ladder, one, nothing))
            chosen = jnp.concatenate(columns, axis=1)
            found = jnp.dot(table_ref[...], chosen, preferred_element_type=jnp.float32)
            high = jnp.broadcast_to(highs[vec : vec + 1, :], (coeffs, targets))
            value = jnp.zeros((coeffs, targets), jnp.float32)
            for seg in range(segs):
                value = jnp.where(high == seg, found[seg * coeffs : (seg + 1) * coeffs], value)
            for tile in range(tiles):
                picks_ref[tile, pl.ds(base + vec, coeffs, stride=vec_rows), :] = value[
                    :, tile * LANES : (tile + 1) * LANES
                ]
        return carry

    lax.fori_loop(0, vec_rows // STEP, pick, 0)

    def contract(at, carry):
        total = acc_ref[...]
        for step in range(4):
            coeff = at * 4 + step
            base = pl.multiple_of(coeff * vec_rows, STEP)
            block = jnp.concatenate(
                [picks_ref[tile, pl.ds(base, vec_rows), :] for tile in range(tiles)], axis=1
            )
            total += jnp.dot(
                ops_ref[coeff],
                block.astype(jnp.bfloat16)[:vecs],
                preferred_element_type=jnp.float32,
            )
        acc_ref[...] = total
        return carry

    lax.fori_loop(0, coeffs // 4, contract, 0)
    out_ref[...] = acc_ref[...]

    coarse_segs = coarse_ref.shape[0] // LANES
    for seg in range(coarse_segs):
        coarse_table_ref[:, seg * LANES : (seg + 1) * LANES] = jnp.transpose(
            coarse_ref[seg * LANES : (seg + 1) * LANES, :]
        )
    pieces = spread_lists(coarse_idx_ref[...], coarse_pos_ref[...])
    lows = [piece & (LANES - 1) for piece in pieces]
    highs = [piece >> 7 for piece in pieces]

    def coarse_step(at, total):
        base = pl.multiple_of(at * STEP, STEP)
        block = coarse_table_ref[pl.ds(base, STEP), :]
        for coeff in range(STEP):
            columns = []
            for low, high in zip(lows, highs):
                value = jnp.zeros(low.shape, jnp.float32)
                for seg in range(coarse_segs):
                    row = block[coeff : coeff + 1, seg * LANES : (seg + 1) * LANES]
                    other = gather_lanes(jnp.broadcast_to(row, low.shape), low)
                    value = jnp.where(high == seg, other, value)
                columns.append(value)
            picked = jnp.concatenate(columns, axis=1)[:, :vecs].astype(jnp.bfloat16)
            total += lax.dot_general(
                picked,
                ops_ref[base + coeff],
                (((1,), (1,)), ((), ())),
                preferred_element_type=jnp.float32,
            )
        return total

    coarse_out_ref[...] = lax.fori_loop(
        0, coeffs // STEP, coarse_step, jnp.zeros(coarse_out_ref.shape, jnp.float32)
    )


def leaf_far(idx, positions, table, coarse_idx, coarse_positions, coarse, ops):
    coeffs, _, vecs = ops.shape
    targets = idx.shape[1]
    vec_lanes = positions.shape[1]
    vec_rows = round_up(vecs, 16)
    return pl.pallas_call(
        leaf_kernel,
        out_shape=(
            jax.ShapeDtypeStruct((coeffs, targets), jnp.float32),
            jax.ShapeDtypeStruct((coarse_idx.shape[0], coeffs), jnp.float32),
        ),
        in_specs=[pl.BlockSpec(memory_space=pltpu.VMEM)] * 7,
        out_specs=[pl.BlockSpec(memory_space=pltpu.VMEM)] * 2,
        scratch_shapes=[
            pltpu.VMEM((vec_lanes, targets), jnp.float32),
            pltpu.VMEM((vec_lanes, targets), jnp.int32),
            pltpu.VMEM((targets // LANES, coeffs * vec_rows, LANES), jnp.float32),
            pltpu.VMEM((coeffs, targets), jnp.float32),
            pltpu.VMEM((LANES, coarse.shape[0]), jnp.float32),
        ],
        compiler_params=pltpu.CompilerParams(vmem_limit_bytes=48 * 1024 * 1024),
        cost_estimate=pl.CostEstimate(
            flops=20_000_000_000, bytes_accessed=4_000_000, transcendentals=0
        ),
        name="leaf_far",
    )(idx, positions, table, coarse_idx, coarse_positions, coarse, ops)


def upward(children, m2m_ops):
    grouped = children.reshape(-1, 8, children.shape[-1])
    return jnp.einsum("noc,ocd->nd", grouped, m2m_ops, precision=lax.Precision.HIGHEST)


def downward(parents, l2l_ops):
    spread = jnp.einsum("nc,ocd->nod", parents, l2l_ops, precision=lax.Precision.HIGHEST)
    return spread.reshape(-1, parents.shape[-1])


def per_device(
    multipoles,
    list_src,
    list_mask,
    send_boxes,
    send_count,
    coarse_src,
    coarse_mask,
    m2l_ops,
    m2m_ops,
    l2l_ops,
):
    boxes, coeffs = multipoles.shape
    entries = list_src.shape[1]
    vecs = m2l_ops.shape[0]
    count_leaf = lax.axis_size("leaf")
    count_sub = lax.axis_size("sub")
    capacity = send_boxes.shape[2]
    bits = count_leaf.bit_length() - 1
    me = lax.axis_index("leaf")
    chip = boxes * count_sub
    members = count_leaf * count_sub
    segs = count_sub + 1
    by_coeff = multipoles.T

    current = multipoles.astype(jnp.float32)
    for level_step in range(LEVELS):
        current = upward(current, m2m_ops)
    count_coarse = current.shape[0]
    height = round_up(count_coarse + 1, 8)
    coarse_rows = current.astype(jnp.bfloat16).astype(jnp.float32)
    coarse_rows = jnp.pad(
        coarse_rows, ((0, height - count_coarse), (0, LANES - coeffs))
    )
    table, all_coarse = exchange(
        by_coeff, send_boxes[0], send_count, coarse_rows, members, bits
    )

    entry_lanes = round_up(entries + 1, LANES)
    vec_lanes = round_up(vecs, LANES)
    positions = list_positions(vec_lanes, entry_lanes - 1)
    source = list_src.T
    remote = source - chip
    distance = jnp.bitwise_xor(remote // capacity, me)
    which = jnp.zeros_like(distance)
    for bit in range(1, bits):
        which += (distance >= (1 << bit)).astype(jnp.int32)
    row = jnp.where(source < chip, source, chip + which * capacity + remote % capacity)
    row = jnp.where(list_mask.T > 0, row, segs * boxes)
    row = jnp.pad(
        row, ((0, entry_lanes - entries), (0, 0)), constant_values=segs * boxes
    )

    all_coarse = all_coarse.reshape(members * height, LANES)
    all_coarse = jnp.pad(
        all_coarse, ((0, round_up(members * height, LANES) - members * height), (0, 0))
    )
    coarse_row = coarse_src // count_coarse * height + coarse_src % count_coarse
    coarse_row = jnp.where(coarse_mask > 0, coarse_row, count_coarse)
    coarse_row = jnp.pad(
        coarse_row,
        ((0, height - count_coarse), (0, entry_lanes - entries)),
        constant_values=count_coarse,
    )
    first_coarse = lax.axis_index(("leaf", "sub")) * count_coarse
    doubled = jnp.asarray(np.concatenate([positions, positions], axis=0))
    coarse_positions = lax.dynamic_slice_in_dim(doubled, first_coarse % 8, height, 0)
    far_leaf, inherited = leaf_far(
        row,
        jnp.asarray(positions),
        table,
        coarse_row,
        coarse_positions,
        all_coarse,
        m2l_ops.transpose(1, 2, 0),
    )
    inherited = inherited[:count_coarse]
    for level_step in range(LEVELS):
        inherited = downward(inherited, l2l_ops)
    return far_leaf.T + inherited


def solution(mesh):
    placed = (
        P(("groups", "leaf", "sub"), None),
        P(("groups", "leaf", "sub"), None),
        P(("groups", "leaf", "sub"), None),
        P(("groups", "leaf", "sub"), None, None),
        P(("groups", "leaf", "sub"), None),
        P(("groups", "leaf", "sub"), None),
        P(("groups", "leaf", "sub"), None),
        P(),
        P(),
        P(),
    )
    return jax.shard_map(
        per_device,
        mesh=mesh,
        in_specs=placed,
        out_specs=P(("groups", "leaf", "sub"), None),
        check_vma=False,
    )
```

time: 85.4 us -> 55.5 us (0.65)
  blocking collectives: 19.6 us -> 0 us
  Pallas kernels: 24.3 us -> 42.8 us
  local copies, waits for them, and re-layouts: 24.8 us -> 6.54 us
  starting transfers between devices: 7.1 us -> 0 us
  other arithmetic: 4.9 us -> 2.65 us
  matrix products: 3.85 us -> 2.94 us
    all_gather x2 -> x0, blocking collectives: 19.6 us -> none  [the longest x1 17.6 us: per_device(): lax.all_gather(coarse_rows, ('leaf', 'sub'), axis=0, tiled=True)]
    pallas_call x2, Pallas kernels: 24.3 us -> 42.8 us  [the longest x1 33 us: leaf_far(): pl.pallas_call(leaf_kernel, out_shape=(jax.ShapeDtypeStruct((coeffs, targ...]
    ppermute x3 -> x0, starting transfers between devices: 7.1 us -> none  [per_device(): incoming.append(lax.ppermute(part, 'leaf', pairs))]
    unnamed x21 -> x13, local copies, waits for them, and re-layouts: 12.2 us -> 5.57 us
    pad x1 -> x0, local copies, waits for them, and re-layouts: 6.17 us -> none  [per_device(): ops = jnp.pad(m2l_ops, ((0, steps * STEP - vecs), (0, 0), (0, 0)))]
    reshape x1 -> x0, local copies, waits for them, and re-layouts: 4.73 us -> none  [per_device(): ops = ops.reshape(steps, coeffs, STEP * coeffs)]
    reduce_sum x2 -> x0, other arithmetic: 1.61 us -> none  [the longest x1 0.84 us: per_device(): limit = jnp.sum(jnp.where(is_peer, send_count[0][None], 0), axis=1)]
    dot_general x1 -> x0, matrix products: 0.91 us -> none  [per_device(): jnp.dot(by_coeff, chosen, preferred_element_type=multipoles.dtype)]
  transfers between devices with their start and end apart: 3 -> 0, of which waited for: 0 -> 0; matrix products, arithmetic and copies ran while one was open for 32% -> 0% of each run, Pallas kernels for 3% -> 0%
where the time goes in v2:
time: 55.5 us; the launch traced here: 55 us
  Pallas kernels  42.8 us (77%)
  local copies, waits for them, and re-layouts  6.54 us (12%)
  matrix products  2.94 us (5%)
  other arithmetic  2.65 us (5%)
    pallas_call x1, Pallas kernels, leaf_far(): pl.pallas_call(leaf_kernel, out_shape=(jax.ShapeDtypeStruct((coeffs, targ...  33 us
    pallas_call x1, Pallas kernels, exchange(): pl.pallas_call(exchange_kernel, out_shape=(jax.ShapeDtypeStruct((3 * coef...  9.8 us
    unnamed x13, local copies, waits for them, and re-layouts  5.57 us
    dot_general x2, matrix products, upward(): jnp.einsum('noc,ocd->nd', grouped, m2m_ops, precision=lax.Precision.HIGHEST)  2.41 us
    select_n x1, other arithmetic, per_device(): row = jnp.where(list_mask.T > 0, row, segs * boxes)  1.28 us

profile of v2, /device:TPU:0, one launch (start us, length us, event | category | flops | bytes accessed | tf_op | source)
XLA Modules:
  0.0 55.0 jit_solution(6605883957042406235)
XLA Ops:
  0.0 0.0 copy-start
  0.0 0.8 %constant_dynamic-slice_fusion.coarse_pos_ref = s32[8,384]{1,0:T(8,128)S(1)} fusion(s32[16,384]{1,0:T(8,128)} %constant.93.clone, s32[]{:T(128)S(6)} %select_n.51), kind=kLoop, calls=%fused_computation.39 | loop fusion | bytes 24580 | tf_op jit(solution)/shard_map/dynamic_slice | solution.py:385
  0.8 1.3 %fusion.5 = s32[189,256]{1,0:T(8,128)S(1)} fusion(s32[256,189]{0,1:T(8,128)} %param.13, s32[256,189]{0,1:T(8,128)} %param.14, s32[]{:T(128)S(6)} %axis_index.27), kind=kLoop, calls=%fused_computation.12 | loop fusion | flops 1596672 | bytes 580612 | tf_op jit(solution)/shard_map/jit(_where)/select_n | solution.py:367
  2.1 0.9 %copy.14 = bf16[256,64]{1,0:T(8,128)(2,1)S(1)} copy(bf16[256,64]{0,1:T(8,128)(2,1)} %param.12) | data formatting | bytes 65536 | tf_op args[0]
  3.0 1.2 %fusion.1 = f32[4,8,64,1]{2,1,3,0:T(8,128)S(1)} fusion(f32[8,64,64]{2,1,0:T(8,128)} %param.20, bf16[4,8,64,8]{2,3,1,0:T(8,128)(2,1)S(1)} %bitcast.47), kind=kOutput, calls=%fused_computation.8 | convolution fusion | flops 12582912 | bytes 172032 | tf_op jit(solution)/shard_map/noc,ocd->nd/dot_general | solution.py:311
  4.2 1.2 %fusion = bf16[4,64]{1,0:T(4,128)(2,1)S(1)} fusion(f32[8,64,64]{2,1,0:T(8,128)} %param.20, f32[4,8,64,1]{2,1,3,0:T(8,128)S(1)} %fusion.1), kind=kOutput, calls=%fused_computation.1 | convolution fusion | flops 1573120 | bytes 139776 | tf_op jit(solution)/shard_map/noc,ocd->nd/dot_general | solution.py:311
  5.4 0.0 copy-start.1
  5.4 0.8 %copy-done.1 = bf16[256,64]{0,1:T(8,128)(2,1)S(1)} copy-done((bf16[256,64]{0,1:T(8,128)(2,1)S(1)}, bf16[256,64]{0,1:T(8,128)(2,1)}, u32[]{:S(2)}) %copy-start.1) | copy-done | bytes 32792
  6.2 0.0 copy-start.2
  6.2 0.7 %copy-done.2 = s32[1,8,16]{2,1,0:T(8,128)S(1)} copy-done((s32[1,8,16]{2,1,0:T(8,128)S(1)}, s32[1,8,16]{2,1,0:T(8,128)}, u32[]{:S(2)}) %copy-start.2) | copy-done | bytes 536
  6.9 0.0 copy-start.3
  6.9 0.7 %copy-done.3 = s32[1,8]{1,0:T(1,128)S(1)} copy-done((s32[1,8]{1,0:T(1,128)S(1)}, s32[1,8]{1,0:T(1,128)}, u32[]{:S(2)}) %copy-start.3) | copy-done | bytes 56
  7.5 9.8 %exchange.1 = (bf16[192,256]{1,0:T(8,128)(2,1)S(1)}, f32[16,8,128]{2,1,0:T(8,128)S(1)}) custom-call(bf16[64,256]{1,0:T(8,128)(2,1)S(1)} %bitcast.42, s32[8,16]{1,0:T(8,128)S(1)} %bitcast.43, s32[1,8]{1,0:T(1,128)S(1)} %copy-done.3, f32[8,128]{1,0:T(8,128)S(1)} %pad_convert_fusion.coarse_ref), custom_call_target="tpu_custom_call" | custom-call | tf_op jit(solution)/shard_map/exchange/pallas_call | solution.py:157
  17.3 0.7 %fusion.15 = s32[4,189]{1,0:T(4,128)S(1)} fusion(s32[4,189]{1,0:T(4,128)} %param.17, s32[4,189]{1,0:T(4,128)} %param.18), kind=kLoop, calls=%fused_computation.31 | loop fusion | flops 17388 | bytes 9072 | tf_op jit(solution)/shard_map/jit(_where)/select_n | solution.py:377
  18.1 0.0 copy-start.4
  18.1 1.9 %copy-done.4 = bf16[316,64,64]{0,2,1:T(8,128)(2,1)S(1)} copy-done((bf16[316,64,64]{0,2,1:T(8,128)(2,1)S(1)}, bf16[316,64,64]{0,2,1:T(8,128)(2,1)}, u32[]{:S(2)}) %copy-start.4) | copy-done | bytes 2588696
  20.0 0.7 %copy-done.5 = s32[8,384]{1,0:T(8,128)S(1)} copy-done((s32[8,384]{1,0:T(8,128)S(1)}, s32[8,384]{1,0:T(8,128)}, u32[]{:S(2)}) %copy-start.5) | copy-done | bytes 12312
  20.7 33.0 %leaf_far.1 = (f32[64,256]{1,0:T(8,128)S(1)}, f32[8,64]{1,0:T(8,128)S(1)}) custom-call(s32[256,256]{1,0:T(8,128)S(1)} %pad.14.idx_ref, s32[8,384]{1,0:T(8,128)S(1)} %copy-done.5, bf16[192,256]{1,0:T(8,128)(2,1)S(1)} %get-tuple-element.9.table_ref, s32[8,256]{1,0:T(8,128)S(1)} %pad.17.coarse_idx_ref, s32[8,384]{1,0:T(8,128)S(1)} %constant_dynamic-slice_fusion.coarse_pos_ref, ...), custom_call_target="tpu_custom_call" | custom-call | flops 20000000000 | bytes 4000000 | tf_op jit(solution)/shard_map/leaf_far/pallas_call | solution.py:286
  53.7 0.0 copy-done
  53.7 0.3 fusion.18
  53.9 0.3 fusion.8
  54.2 0.1 copy.31
  54.3 0.1 copy.17
  54.4 0.6 %bitcast_add_fusion.1 = f32[256,64]{0,1:T(8,128)} fusion(f32[256,64]{0,1:T(8,128)S(1)} %copy.17, f32[64,256]{1,0:T(8,128)S(1)} %get-tuple-element.11), kind=kLoop, calls=%fused_computation.17 | loop fusion | flops 16384 | bytes 196608 | tf_op jit(solution)/shard_map/add | solution.py:398
  (4 shorter events, 0.0 us)
Async XLA Ops:
  0.0 53.7 %copy-start = (f32[8,64,64]{2,1,0:T(8,128)S(1)}, f32[8,64,64]{2,1,0:T(8,128)}, u32[]{:S(2)}) copy-start(f32[8,64,64]{2,1,0:T(8,128)} %param.21) | copy-start | bytes 393220
  5.4 0.8 %copy-start.1 = (bf16[256,64]{0,1:T(8,128)(2,1)S(1)}, bf16[256,64]{0,1:T(8,128)(2,1)}, u32[]{:S(2)}) copy-start(bf16[256,64]{0,1:T(8,128)(2,1)} %param.12) | copy-start | bytes 98308
  6.2 0.7 %copy-start.2 = (s32[1,8,16]{2,1,0:T(8,128)S(1)}, s32[1,8,16]{2,1,0:T(8,128)}, u32[]{:S(2)}) copy-start(s32[1,8,16]{2,1,0:T(8,128)} %param.15) | copy-start | bytes 1540
  6.9 0.7 %copy-start.3 = (s32[1,8]{1,0:T(1,128)S(1)}, s32[1,8]{1,0:T(1,128)}, u32[]{:S(2)}) copy-start(s32[1,8]{1,0:T(1,128)} %counts_ref.1) | copy-start | bytes 100
  18.1 1.9 %copy-start.4 = (bf16[316,64,64]{0,2,1:T(8,128)(2,1)S(1)}, bf16[316,64,64]{0,2,1:T(8,128)(2,1)}, u32[]{:S(2)}) copy-start(bf16[316,64,64]{0,2,1:T(8,128)(2,1)} %param.19) | copy-start | bytes 7766020
  20.0 0.7 %copy-start.5 = (s32[8,384]{1,0:T(8,128)S(1)}, s32[8,384]{1,0:T(8,128)}, u32[]{:S(2)}) copy-start(s32[8,384]{1,0:T(8,128)} %constant.94.clone.pos_ref) | copy-start | bytes 36868

commit v3 on v2

--- a/solution.py
+++ b/solution.py
@@ -29,6 +29,46 @@
                         table[octant, vector_rank[step_x, step_y, step_z]] = entry
                         entry += 1
     return table
+
+
+def step_plan():
+    vector_rank = {}
+    for step_x in range(-3, 4):
+        for step_y in range(-3, 4):
+            for step_z in range(-3, 4):
+                if max(abs(step_x), abs(step_y), abs(step_z)) > 1:
+                    vector_rank[step_x, step_y, step_z] = len(vector_rank)
+    groups = []
+    for axes in ((), (0,), (1,), (2,), (0, 1), (0, 2), (1, 2), (0, 1, 2)):
+        steps = []
+        spans = [(3,) if axis in axes else range(-2, 3) for axis in range(3)]
+        for inner in np.ndindex(*[len(span) for span in spans]):
+            vector = [span[place] for span, place in zip(spans, inner)]
+            if max(abs(part) for part in vector) < 2:
+                continue
+            ranks = []
+            for choice in range(1 << len(axes)):
+                signed = list(vector)
+                for place, axis in enumerate(axes):
+                    signed[axis] = -3 if choice >> place & 1 else 3
+                ranks.append(vector_rank[tuple(signed)])
+            steps.append(ranks)
+        groups.append((axes, steps))
+    return groups
+
+
+def step_tables(positions, lanes, dead):
+    entries = np.full((8, lanes), dead, np.int32)
+    ranks = np.zeros((lanes, 8), np.int32)
+    at = 0
+    for axes, steps in step_plan():
+        for step in steps:
+            for octant in range(8):
+                choice = sum((octant >> axis & 1) << place for place, axis in enumerate(axes))
+                entries[octant, at] = positions[octant, step[choice]]
+            ranks[at, : len(step)] = step
+            at += 1
+    return entries, ranks
 
 
 def round_up(value, unit):
@@ -178,64 +218,91 @@
 
 
 def leaf_kernel(
-    idx_ref, pos_ref, table_ref, coarse_idx_ref, coarse_pos_ref, coarse_ref, ops_ref,
-    out_ref, coarse_out_ref, low_ref, high_ref, picks_ref, acc_ref, coarse_table_ref,
+    idx_ref, pos_ref, ranks_ref, table_ref, coarse_idx_ref, coarse_pos_ref, coarse_ref, ops_hbm,
+    out_ref, coarse_out_ref, low_ref, high_ref, picks_ref, acc_ref, coarse_table_ref, ops_ref,
+    ops_sem,
 ):
+    ops_copy = pltpu.make_async_copy(ops_hbm, ops_ref, ops_sem)
+    ops_copy.start()
     coeffs, _, vecs = ops_ref.shape
     targets = idx_ref.shape[1]
     width = table_ref.shape[1]
     segs = table_ref.shape[0] // coeffs
-    vec_rows = picks_ref.shape[1] // coeffs
+    pitch = picks_ref.shape[1] // coeffs
+    vec_rows = pitch - 1
     tiles = targets // LANES
     rows = jnp.transpose(idx_ref[...])
     where = jnp.concatenate([pos_ref[...]] * (targets // 8), axis=0)
     for out, piece in enumerate(spread_lists(rows, where)):
         block = jnp.transpose(piece)
-        low_ref[out * LANES : (out + 1) * LANES, :] = (block % width).astype(jnp.float32)
-        high_ref[out * LANES : (out + 1) * LANES, :] = block // width
+        low = (block % width).astype(jnp.float32)
+        high = block // width
+        for tile in range(tiles):
+            lanes = slice(tile * LANES, (tile + 1) * LANES)
+            low_ref[tile, out * LANES : (out + 1) * LANES, :] = low[:, lanes]
+            high_ref[tile, out * LANES : (out + 1) * LANES, :] = high[:, lanes]
+    for row in range(vecs, vec_rows):
+        for tile in range(tiles):
+            picks_ref[tile, pl.ds(row, coeffs, stride=pitch), :] = jnp.zeros(
+                (coeffs, LANES), jnp.float32
+            )
     acc_ref[...] = jnp.zeros_like(acc_ref)
     ladder = lax.broadcasted_iota(jnp.int32, (width, LANES), 0).astype(jnp.float32)
     ladder = ladder.astype(jnp.bfloat16)
     one = jnp.ones((), jnp.bfloat16)
     nothing = jnp.zeros((), jnp.bfloat16)
-
-    def pick(at, carry):
-        base = pl.multiple_of(at * STEP, STEP)
-        lows = low_ref[pl.ds(base, STEP), :]
-        highs = high_ref[pl.ds(base, STEP), :]
-        for vec in range(STEP):
-            columns = []
-            for tile in range(tiles):
-                low = lows[vec : vec + 1, tile * LANES : (tile + 1) * LANES]
-                low = jnp.broadcast_to(low, (16, LANES)).astype(jnp.bfloat16)
-                low = jnp.concatenate([low] * (width // 16), axis=0)
-                columns.append(jnp.where(low == ladder, one, nothing))
-            chosen = jnp.concatenate(columns, axis=1)
-            found = jnp.dot(table_ref[...], chosen, preferred_element_type=jnp.float32)
-            high = jnp.broadcast_to(highs[vec : vec + 1, :], (coeffs, targets))
-            value = jnp.zeros((coeffs, targets), jnp.float32)
+    octants = lax.broadcasted_iota(jnp.int32, (coeffs, LANES), 1) & 7
+
+    def pick(at, axes):
+        columns = []
+        for tile in range(tiles):
+            low = jnp.broadcast_to(low_ref[tile, pl.ds(at, 1), :], (16, LANES))
+            low = jnp.concatenate([low.astype(jnp.bfloat16)] * (width // 16), axis=0)
+            columns.append(jnp.where(low == ladder, one, nothing))
+        chosen = jnp.concatenate(columns, axis=1)
+        found = jnp.dot(table_ref[...], chosen, preferred_element_type=jnp.float32)
+        bits = jnp.zeros_like(octants)
+        for place, axis in enumerate(axes):
+            bits += ((octants >> axis) & 1) << place
+        for tile in range(tiles):
+            high = jnp.broadcast_to(high_ref[tile, pl.ds(at, 1), :], (coeffs, LANES))
+            value = jnp.zeros((coeffs, LANES), jnp.float32)
             for seg in range(segs):
-                value = jnp.where(high == seg, found[seg * coeffs : (seg + 1) * coeffs], value)
-            for tile in range(tiles):
-                picks_ref[tile, pl.ds(base + vec, coeffs, stride=vec_rows), :] = value[
-                    :, tile * LANES : (tile + 1) * LANES
+                part = found[
+                    seg * coeffs : (seg + 1) * coeffs, tile * LANES : (tile + 1) * LANES
                 ]
-        return carry
-
-    lax.fori_loop(0, vec_rows // STEP, pick, 0)
+                value = jnp.where(high == seg, part, value)
+            for choice in range(1 << len(axes)):
+                kept = jnp.where(bits == choice, value, 0.0) if axes else value
+                rank = ranks_ref[at, choice]
+                picks_ref[tile, pl.ds(rank, coeffs, stride=pitch), :] = kept
+
+    first = 0
+    for axes, steps in step_plan():
+        unroll = next(n for n in (7, 5, 1) if len(steps) % n == 0)
+
+        def several(turn, carry, axes=axes, first=first, unroll=unroll):
+            for inner in range(unroll):
+                pick(first + turn * unroll + inner, axes)
+            return carry
+
+        lax.fori_loop(0, len(steps) // unroll, several, 0)
+        first += len(steps)
+    ops_copy.wait()
 
     def contract(at, carry):
         total = acc_ref[...]
         for step in range(4):
             coeff = at * 4 + step
-            base = pl.multiple_of(coeff * vec_rows, STEP)
             block = jnp.concatenate(
-                [picks_ref[tile, pl.ds(base, vec_rows), :] for tile in range(tiles)], axis=1
+                [
+                    picks_ref[tile, pl.ds(coeff * pitch, vec_rows), :].astype(jnp.bfloat16)
+                    for tile in range(tiles)
+                ],
+                axis=1,
             )
             total += jnp.dot(
-                ops_ref[coeff],
-                block.astype(jnp.bfloat16)[:vecs],
-                preferred_element_type=jnp.float32,
+                ops_ref[coeff], block[:vecs], preferred_element_type=jnp.float32
             )
         acc_ref[...] = total
         return carry
@@ -278,10 +345,10 @@
     )
 
 
-def leaf_far(idx, positions, table, coarse_idx, coarse_positions, coarse, ops):
+def leaf_far(idx, positions, ranks, table, coarse_idx, coarse_positions, coarse, ops):
     coeffs, _, vecs = ops.shape
     targets = idx.shape[1]
-    vec_lanes = positions.shape[1]
+    step_lanes = positions.shape[1]
     vec_rows = round_up(vecs, 16)
     return pl.pallas_call(
         leaf_kernel,
@@ -289,21 +356,32 @@
             jax.ShapeDtypeStruct((coeffs, targets), jnp.float32),
             jax.ShapeDtypeStruct((coarse_idx.shape[0], coeffs), jnp.float32),
         ),
-        in_specs=[pl.BlockSpec(memory_space=pltpu.VMEM)] * 7,
+        in_specs=[
+            pl.BlockSpec(memory_space=pltpu.VMEM),
+            pl.BlockSpec(memory_space=pltpu.VMEM),
+            pl.BlockSpec(memory_space=pltpu.SMEM),
+            pl.BlockSpec(memory_space=pltpu.VMEM),
+            pl.BlockSpec(memory_space=pltpu.VMEM),
+            pl.BlockSpec(memory_space=pltpu.VMEM),
+            pl.BlockSpec(memory_space=pltpu.VMEM),
+            pl.BlockSpec(memory_space=pl.ANY),
+        ],
         out_specs=[pl.BlockSpec(memory_space=pltpu.VMEM)] * 2,
         scratch_shapes=[
-            pltpu.VMEM((vec_lanes, targets), jnp.float32),
-            pltpu.VMEM((vec_lanes, targets), jnp.int32),
-            pltpu.VMEM((targets // LANES, coeffs * vec_rows, LANES), jnp.float32),
+            pltpu.VMEM((targets // LANES, step_lanes, LANES), jnp.float32),
+            pltpu.VMEM((targets // LANES, step_lanes, LANES), jnp.int32),
+            pltpu.VMEM((targets // LANES, coeffs * (vec_rows + 1), LANES), jnp.float32),
             pltpu.VMEM((coeffs, targets), jnp.float32),
             pltpu.VMEM((LANES, coarse.shape[0]), jnp.float32),
+            pltpu.VMEM(ops.shape, ops.dtype),
+            pltpu.SemaphoreType.DMA,
         ],
         compiler_params=pltpu.CompilerParams(vmem_limit_bytes=48 * 1024 * 1024),
         cost_estimate=pl.CostEstimate(
             flops=20_000_000_000, bytes_accessed=4_000_000, transcendentals=0
         ),
         name="leaf_far",
-    )(idx, positions, table, coarse_idx, coarse_positions, coarse, ops)
+    )(idx, positions, ranks, table, coarse_idx, coarse_positions, coarse, ops)
 
 
 def upward(children, m2m_ops):
@@ -357,6 +435,7 @@
     entry_lanes = round_up(entries + 1, LANES)
     vec_lanes = round_up(vecs, LANES)
     positions = list_positions(vec_lanes, entry_lanes - 1)
+    step_entries, ranks = step_tables(positions, entry_lanes, entry_lanes - 1)
     source = list_src.T
     remote = source - chip
     distance = jnp.bitwise_xor(remote // capacity, me)
@@ -385,7 +464,8 @@
     coarse_positions = lax.dynamic_slice_in_dim(doubled, first_coarse % 8, height, 0)
     far_leaf, inherited = leaf_far(
         row,
-        jnp.asarray(positions),
+        jnp.asarray(step_entries),
+        jnp.asarray(ranks),
         table,
         coarse_row,
         coarse_positions,

time: 55.5 us -> 44.2 us (0.80)
  Pallas kernels: 42.8 us -> 30.6 us
  local copies, waits for them, and re-layouts: 6.54 us -> 7.43 us
    pallas_call x1, Pallas kernels: 33 us -> 20.8 us  [leaf_far(): pl.pallas_call(leaf_kernel, out_shape=(jax.ShapeDtypeStruct((coeffs, targ...]
    unnamed x13 -> x15, local copies, waits for them, and re-layouts: 5.57 us -> 6.46 us
where the time goes in v3:
time: 44.2 us; the launch traced here: 43.7 us
  Pallas kernels  30.6 us (69%)
  local copies, waits for them, and re-layouts  7.43 us (17%)
  matrix products  2.92 us (7%)
  other arithmetic  2.65 us (6%)
    pallas_call x1, Pallas kernels, leaf_far(): pl.pallas_call(leaf_kernel, out_shape=(jax.ShapeDtypeStruct((coeffs, targ...  20.8 us
    pallas_call x1, Pallas kernels, exchange(): pl.pallas_call(exchange_kernel, out_shape=(jax.ShapeDtypeStruct((3 * coef...  9.8 us
    unnamed x15, local copies, waits for them, and re-layouts  6.46 us
    dot_general x2, matrix products, upward(): jnp.einsum('noc,ocd->nd', grouped, m2m_ops, precision=lax.Precision.HIGHEST)  2.41 us
    select_n x1, other arithmetic, per_device(): row = jnp.where(list_mask.T > 0, row, segs * boxes)  1.28 us

profile of v3, /device:TPU:0, one launch (start us, length us, event | category | flops | bytes accessed | tf_op | source)
XLA Modules:
  0.0 43.7 jit_solution(13054076117639900348)
XLA Ops:
  0.0 0.0 copy-start
  0.0 0.8 %constant_dynamic-slice_fusion.coarse_pos_ref = s32[8,384]{1,0:T(8,128)S(1)} fusion(s32[16,384]{1,0:T(8,128)} %constant.95.clone, s32[]{:T(128)S(6)} %select_n.51), kind=kLoop, calls=%fused_computation.39 | loop fusion | bytes 24580 | tf_op jit(solution)/shard_map/dynamic_slice | solution.py:464
  0.8 1.3 %fusion.5 = s32[189,256]{1,0:T(8,128)S(1)} fusion(s32[256,189]{0,1:T(8,128)} %param.14, s32[256,189]{0,1:T(8,128)} %param.15, s32[]{:T(128)S(6)} %axis_index.27), kind=kLoop, calls=%fused_computation.12 | loop fusion | flops 1596672 | bytes 580612 | tf_op jit(solution)/shard_map/jit(_where)/select_n | solution.py:446
  2.1 0.9 %copy.15 = bf16[256,64]{1,0:T(8,128)(2,1)S(1)} copy(bf16[256,64]{0,1:T(8,128)(2,1)} %param.13) | data formatting | bytes 65536 | tf_op args[0]
  3.0 1.2 %fusion.1 = f32[4,8,64,1]{2,1,3,0:T(8,128)S(1)} fusion(f32[8,64,64]{2,1,0:T(8,128)} %param.21, bf16[4,8,64,8]{2,3,1,0:T(8,128)(2,1)S(1)} %bitcast.47), kind=kOutput, calls=%fused_computation.8 | convolution fusion | flops 12582912 | bytes 172032 | tf_op jit(solution)/shard_map/noc,ocd->nd/dot_general | solution.py:389
  4.2 1.2 %fusion = bf16[4,64]{1,0:T(4,128)(2,1)S(1)} fusion(f32[8,64,64]{2,1,0:T(8,128)} %param.21, f32[4,8,64,1]{2,1,3,0:T(8,128)S(1)} %fusion.1), kind=kOutput, calls=%fused_computation.1 | convolution fusion | flops 1573120 | bytes 139776 | tf_op jit(solution)/shard_map/noc,ocd->nd/dot_general | solution.py:389
  5.4 0.0 copy-start.1
  5.4 0.8 %copy-done.1 = bf16[256,64]{0,1:T(8,128)(2,1)S(1)} copy-done((bf16[256,64]{0,1:T(8,128)(2,1)S(1)}, bf16[256,64]{0,1:T(8,128)(2,1)}, u32[]{:S(2)}) %copy-start.1) | copy-done | bytes 32792
  6.2 0.0 copy-start.2
  6.2 0.7 %copy-done.2 = s32[1,8,16]{2,1,0:T(8,128)S(1)} copy-done((s32[1,8,16]{2,1,0:T(8,128)S(1)}, s32[1,8,16]{2,1,0:T(8,128)}, u32[]{:S(2)}) %copy-start.2) | copy-done | bytes 536
  6.9 0.7 %copy-done.3 = s32[1,8]{1,0:T(1,128)S(1)} copy-done((s32[1,8]{1,0:T(1,128)S(1)}, s32[1,8]{1,0:T(1,128)}, u32[]{:S(2)}) %copy-start.3) | copy-done | bytes 56
  7.5 9.8 %exchange.1 = (bf16[192,256]{1,0:T(8,128)(2,1)S(1)}, f32[16,8,128]{2,1,0:T(8,128)S(1)}) custom-call(bf16[64,256]{1,0:T(8,128)(2,1)S(1)} %bitcast.42, s32[8,16]{1,0:T(8,128)S(1)} %bitcast.43, s32[1,8]{1,0:T(1,128)S(1)} %copy-done.3, f32[8,128]{1,0:T(8,128)S(1)} %pad_convert_fusion.coarse_ref), custom_call_target="tpu_custom_call" | custom-call | tf_op jit(solution)/shard_map/exchange/pallas_call | solution.py:197
  17.3 0.7 %fusion.15 = s32[4,189]{1,0:T(4,128)S(1)} fusion(s32[4,189]{1,0:T(4,128)} %param.18, s32[4,189]{1,0:T(4,128)} %param.19), kind=kLoop, calls=%fused_computation.31 | loop fusion | flops 17388 | bytes 9072 | tf_op jit(solution)/shard_map/jit(_where)/select_n | solution.py:456
  18.1 0.0 copy-start.4
  18.1 1.9 %copy-done.4 = bf16[316,64,64]{0,2,1:T(8,128)(2,1)S(1)} copy-done((bf16[316,64,64]{0,2,1:T(8,128)(2,1)S(1)}, bf16[316,64,64]{0,2,1:T(8,128)(2,1)}, u32[]{:S(2)}) %copy-start.4) | copy-done | bytes 2588696
  20.0 0.9 %copy-done.5 = s32[256,8]{1,0:T(8,128)S(1)} copy-done((s32[256,8]{1,0:T(8,128)S(1)}, s32[256,8]{1,0:T(8,128)}, u32[]{:S(2)}) %copy-start.5) | copy-done | bytes 8216
  20.9 0.7 %copy-done.6 = s32[8,256]{1,0:T(8,128)S(1)} copy-done((s32[8,256]{1,0:T(8,128)S(1)}, s32[8,256]{1,0:T(8,128)}, u32[]{:S(2)}) %copy-start.6) | copy-done | bytes 8216
  21.6 20.8 %leaf_far.1 = (f32[64,256]{1,0:T(8,128)S(1)}, f32[8,64]{1,0:T(8,128)S(1)}) custom-call(s32[256,256]{1,0:T(8,128)S(1)} %pad.14.idx_ref, s32[8,256]{1,0:T(8,128)S(1)} %copy-done.6, s32[256,8]{1,0:T(8,128)S(1)} %copy-done.5, bf16[192,256]{1,0:T(8,128)(2,1)S(1)} %get-tuple-element.9.table_ref, s32[8,256]{1,0:T(8,128)S(1)} %pad.17.coarse_idx_ref, ...), custom_call_target="tpu_custom_call" | custom-call | flops 20000000000 | bytes 4000000 | tf_op jit(solution)/shard_map/leaf_far/pallas_call | solution.py:353
  42.3 0.0 copy-done
  42.3 0.2 fusion.18
  42.6 0.3 fusion.8
  42.9 0.1 copy.32
  42.9 0.1 copy.18
  43.0 0.6 %bitcast_add_fusion.1 = f32[256,64]{0,1:T(8,128)} fusion(f32[256,64]{0,1:T(8,128)S(1)} %copy.18, f32[64,256]{1,0:T(8,128)S(1)} %get-tuple-element.11), kind=kLoop, calls=%fused_computation.17 | loop fusion | flops 16384 | bytes 196608 | tf_op jit(solution)/shard_map/add | solution.py:478
  (6 shorter events, 0.0 us)
Async XLA Ops:
  0.0 42.3 %copy-start = (f32[8,64,64]{2,1,0:T(8,128)S(1)}, f32[8,64,64]{2,1,0:T(8,128)}, u32[]{:S(2)}) copy-start(f32[8,64,64]{2,1,0:T(8,128)} %param.22) | copy-start | bytes 393220
  5.4 0.8 %copy-start.1 = (bf16[256,64]{0,1:T(8,128)(2,1)S(1)}, bf16[256,64]{0,1:T(8,128)(2,1)}, u32[]{:S(2)}) copy-start(bf16[256,64]{0,1:T(8,128)(2,1)} %param.13) | copy-start | bytes 98308
  6.2 0.7 %copy-start.2 = (s32[1,8,16]{2,1,0:T(8,128)S(1)}, s32[1,8,16]{2,1,0:T(8,128)}, u32[]{:S(2)}) copy-start(s32[1,8,16]{2,1,0:T(8,128)} %param.16) | copy-start | bytes 1540
  6.9 0.7 %copy-start.3 = (s32[1,8]{1,0:T(1,128)S(1)}, s32[1,8]{1,0:T(1,128)}, u32[]{:S(2)}) copy-start(s32[1,8]{1,0:T(1,128)} %counts_ref.1) | copy-start | bytes 100
  18.1 1.9 %copy-start.4 = (bf16[316,64,64]{0,2,1:T(8,128)(2,1)S(1)}, bf16[316,64,64]{0,2,1:T(8,128)(2,1)}, u32[]{:S(2)}) copy-start(bf16[316,64,64]{0,2,1:T(8,128)(2,1)} %param.20) | copy-start | bytes 7766020
  20.0 0.9 %copy-start.5 = (s32[256,8]{1,0:T(8,128)S(1)}, s32[256,8]{1,0:T(8,128)}, u32[]{:S(2)}) copy-start(s32[256,8]{1,0:T(8,128)} %constant.97.clone.ranks_ref) | copy-start | bytes 24580
  20.9 0.7 %copy-start.6 = (s32[8,256]{1,0:T(8,128)S(1)}, s32[8,256]{1,0:T(8,128)}, u32[]{:S(2)}) copy-start(s32[8,256]{1,0:T(8,128)} %constant.96.clone.pos_ref) | copy-start | bytes 24580

commit v4 on v3

--- a/solution.py
+++ b/solution.py
@@ -315,7 +315,8 @@
         coarse_table_ref[:, seg * LANES : (seg + 1) * LANES] = jnp.transpose(
             coarse_ref[seg * LANES : (seg + 1) * LANES, :]
         )
-    pieces = spread_lists(coarse_idx_ref[...], coarse_pos_ref[...])
+    me = lax.axis_index("leaf") * lax.axis_size("sub") + lax.axis_index("sub")
+    pieces = spread_lists(coarse_idx_ref[...], coarse_pos_ref[jnp.bitwise_and(me, 7)])
     lows = [piece & (LANES - 1) for piece in pieces]
     highs = [piece >> 7 for piece in pieces]
 
@@ -376,7 +377,7 @@
             pltpu.VMEM(ops.shape, ops.dtype),
             pltpu.SemaphoreType.DMA,
         ],
-        compiler_params=pltpu.CompilerParams(vmem_limit_bytes=48 * 1024 * 1024),
+        compiler_params=pltpu.CompilerParams(vmem_limit_bytes=60 * 1024 * 1024),
         cost_estimate=pl.CostEstimate(
             flops=20_000_000_000, bytes_accessed=4_000_000, transcendentals=0
         ),
@@ -459,16 +460,16 @@
         ((0, height - count_coarse), (0, entry_lanes - entries)),
         constant_values=count_coarse,
     )
-    first_coarse = lax.axis_index(("leaf", "sub")) * count_coarse
-    doubled = jnp.asarray(np.concatenate([positions, positions], axis=0))
-    coarse_positions = lax.dynamic_slice_in_dim(doubled, first_coarse % 8, height, 0)
+    coarse_positions = np.stack(
+        [np.roll(positions, -(turn * count_coarse), axis=0)[:height] for turn in range(8)]
+    )
     far_leaf, inherited = leaf_far(
         row,
         jnp.asarray(step_entries),
         jnp.asarray(ranks),
         table,
         coarse_row,
-        coarse_positions,
+        jnp.asarray(coarse_positions),
         all_coarse,
         m2l_ops.transpose(1, 2, 0),
     )

time: 44.2 us -> 44.6 us (level)
  local copies, waits for them, and re-layouts: 7.43 us -> 5.71 us
  other arithmetic: 2.65 us -> 3.53 us
  matrix products: 2.92 us -> 3.59 us
  Pallas kernels: 30.6 us -> 31.2 us
    unnamed x15 -> x13, local copies, waits for them, and re-layouts: 6.46 us -> 4.23 us
    add x1, other arithmetic: 0.64 us -> 1.48 us  [per_device(): return far_leaf.T + inherited]
    dynamic_slice x1 -> x0, local copies, waits for them, and re-layouts: 0.79 us -> none  [per_device(): lax.dynamic_slice_in_dim(doubled, first_coarse % 8, height, 0)]
    pad x1, local copies, waits for them, and re-layouts: 0.02 us -> 0.72 us  [per_device(): jnp.pad(row, ((0, entry_lanes - entries), (0, 0)), constant_values=segs *...]
    dot_general x2, matrix products: 0.5 us -> 1.18 us  [downward(): jnp.einsum('nc,ocd->nod', parents, l2l_ops, precision=lax.Precision.HIGHEST)]
    pallas_call x1, Pallas kernels: 20.8 us -> 21.4 us  [leaf_far(): pl.pallas_call(leaf_kernel, out_shape=(jax.ShapeDtypeStruct((coeffs, targ...]
    pad x1, local copies, waits for them, and re-layouts: 0.01 us -> 0.6 us  [per_device(): jnp.pad(coarse_row, ((0, height - count_coarse), (0, entry_lanes - entrie...]
where the time goes in v4:
time: 44.6 us; the launch traced here: 44.1 us
  Pallas kernels  31.2 us (70%)
  local copies, waits for them, and re-layouts  5.71 us (13%)
  matrix products  3.59 us (8%)
  other arithmetic  3.53 us (8%)
    pallas_call x1, Pallas kernels, leaf_far(): pl.pallas_call(leaf_kernel, out_shape=(jax.ShapeDtypeStruct((coeffs, targ...  21.4 us
    pallas_call x1, Pallas kernels, exchange(): pl.pallas_call(exchange_kernel, out_shape=(jax.ShapeDtypeStruct((3 * coef...  9.8 us
    unnamed x13, local copies, waits for them, and re-layouts  4.23 us
    dot_general x2, matrix products, upward(): jnp.einsum('noc,ocd->nd', grouped, m2m_ops, precision=lax.Precision.HIGHEST)  2.41 us
    add x1, other arithmetic, per_device(): return far_leaf.T + inherited  1.48 us
    select_n x1, other arithmetic, per_device(): row = jnp.where(list_mask.T > 0, row, segs * boxes)  1.33 us
    dot_general x2, matrix products, downward(): jnp.einsum('nc,ocd->nod', parents, l2l_ops, precision=lax.Precision.HIGHEST)  1.18 us

profile of v4, /device:TPU:0, one launch (start us, length us, event | category | flops | bytes accessed | tf_op | source)
XLA Modules:
  0.0 44.1 jit_solution(6623647277808900374)
XLA Ops:
  0.0 0.0 copy-start
  0.0 1.3 %fusion.5 = s32[189,256]{1,0:T(8,128)S(1)} fusion(s32[256,189]{0,1:T(8,128)} %param.14, s32[256,189]{0,1:T(8,128)} %param.15, s32[]{:T(128)S(6)} %axis_index.15), kind=kLoop, calls=%fused_computation.12 | loop fusion | flops 1596672 | bytes 580612 | tf_op jit(solution)/shard_map/jit(_where)/select_n | solution.py:447
  1.3 0.7 %pad.14.idx_ref = s32[256,256]{1,0:T(8,128)} pad(s32[189,256]{1,0:T(8,128)S(1)} %fusion.5, s32[]{:T(128)} %constant.77.clone.1), padding=0_67x0_0 | pad | bytes 455684 | tf_op jit(solution)/shard_map/jit(_pad)/pad | solution.py:448
  2.0 0.9 %copy.15 = bf16[256,64]{1,0:T(8,128)(2,1)S(1)} copy(bf16[256,64]{0,1:T(8,128)(2,1)} %param.13) | data formatting | bytes 65536 | tf_op args[0]
  2.9 1.2 %fusion.1 = f32[4,8,64,1]{2,1,3,0:T(8,128)S(1)} fusion(f32[8,64,64]{2,1,0:T(8,128)} %param.21, bf16[4,8,64,8]{2,3,1,0:T(8,128)(2,1)S(1)} %bitcast.46), kind=kOutput, calls=%fused_computation.8 | convolution fusion | flops 12582912 | bytes 172032 | tf_op jit(solution)/shard_map/noc,ocd->nd/dot_general | solution.py:390
  4.1 1.2 %fusion = bf16[4,64]{1,0:T(4,128)(2,1)S(1)} fusion(f32[8,64,64]{2,1,0:T(8,128)} %param.21, f32[4,8,64,1]{2,1,3,0:T(8,128)S(1)} %fusion.1), kind=kOutput, calls=%fused_computation.1 | convolution fusion | flops 1573120 | bytes 139776 | tf_op jit(solution)/shard_map/noc,ocd->nd/dot_general | solution.py:390
  5.4 0.0 copy-start.1
  5.4 0.8 %copy-done.1 = bf16[256,64]{0,1:T(8,128)(2,1)S(1)} copy-done((bf16[256,64]{0,1:T(8,128)(2,1)S(1)}, bf16[256,64]{0,1:T(8,128)(2,1)}, u32[]{:S(2)}) %copy-start.1) | copy-done | bytes 32792
  6.1 0.0 copy-start.2
  6.1 0.7 %copy-done.2 = s32[1,8,16]{2,1,0:T(8,128)S(1)} copy-done((s32[1,8,16]{2,1,0:T(8,128)S(1)}, s32[1,8,16]{2,1,0:T(8,128)}, u32[]{:S(2)}) %copy-start.2) | copy-done | bytes 536
  6.8 0.7 %copy-done.3 = s32[1,8]{1,0:T(1,128)S(1)} copy-done((s32[1,8]{1,0:T(1,128)S(1)}, s32[1,8]{1,0:T(1,128)}, u32[]{:S(2)}) %copy-start.3) | copy-done | bytes 56
  7.5 9.8 %exchange.1 = (bf16[192,256]{1,0:T(8,128)(2,1)S(1)}, f32[16,8,128]{2,1,0:T(8,128)S(1)}) custom-call(bf16[64,256]{1,0:T(8,128)(2,1)S(1)} %bitcast.42, s32[8,16]{1,0:T(8,128)S(1)} %bitcast.43, s32[1,8]{1,0:T(1,128)S(1)} %copy-done.3, f32[8,128]{1,0:T(8,128)S(1)} %pad_convert_fusion.coarse_ref), custom_call_target="tpu_custom_call" | custom-call | tf_op jit(solution)/shard_map/exchange/pallas_call | solution.py:197
  17.3 0.0 copy-start.4
  17.3 0.6 %copy-done.4 = bf16[192,256]{1,0:T(8,128)(2,1)} copy-done((bf16[192,256]{1,0:T(8,128)(2,1)}, bf16[192,256]{1,0:T(8,128)(2,1)S(1)}, u32[]{:S(2)}) %copy-start.4) | copy-done | bytes 98328
  17.9 0.6 %copy-done.5 = f32[16,8,128]{2,1,0:T(8,128)} copy-done((f32[16,8,128]{2,1,0:T(8,128)}, f32[16,8,128]{2,1,0:T(8,128)S(1)}, u32[]{:S(2)}) %copy-start.5) | copy-done | bytes 65560
  18.5 0.7 %fusion.15 = s32[4,189]{1,0:T(4,128)S(1)} fusion(s32[4,189]{1,0:T(4,128)} %param.18, s32[4,189]{1,0:T(4,128)} %param.19), kind=kLoop, calls=%fused_computation.31 | loop fusion | flops 17388 | bytes 9072 | tf_op jit(solution)/shard_map/jit(_where)/select_n | solution.py:457
  19.3 0.6 %pad.17.coarse_idx_ref = s32[8,256]{1,0:T(8,128)} pad(s32[4,189]{1,0:T(4,128)S(1)} %fusion.15, s32[]{:T(128)} %constant.71.clone.1), padding=0_4x0_67 | pad | bytes 11220 | tf_op jit(solution)/shard_map/jit(_pad)/pad | solution.py:458
  19.9 21.4 %leaf_far.1 = (f32[64,256]{1,0:T(8,128)}, f32[8,64]{1,0:T(8,128)}) custom-call(s32[256,256]{1,0:T(8,128)} %pad.14.idx_ref, s32[8,256]{1,0:T(8,128)} %constant.81.clone.pos_ref, s32[256,8]{1,0:T(8,128)} %constant.82.clone.ranks_ref, bf16[192,256]{1,0:T(8,128)(2,1)} %copy-done.4, s32[8,256]{1,0:T(8,128)} %pad.17.coarse_idx_ref, ...), custom_call_target="tpu_custom_call" | custom-call | flops 20000000000 | bytes 4000000 | tf_op jit(solution)/shard_map/leaf_far/pallas_call | solution.py:354
  41.3 0.0 copy-done
  41.3 0.9 %fusion.18 = f32[4,8,64]{2,0,1:T(4,128)S(1)} fusion(f32[8,64,64]{2,1,0:T(8,128)S(1)} %copy-done, f32[8,64]{1,0:T(8,128)} %get-tuple-element.12), kind=kOutput, calls=%fused_computation.35 | convolution fusion | flops 1572864 | bytes 141312 | tf_op jit(solution)/shard_map/nc,ocd->nod/dot_general | solution.py:394
  42.2 0.3 fusion.8
  42.5 0.1 copy.32
  42.5 0.1 copy.18
  42.6 1.5 %bitcast_add_fusion.1 = f32[256,64]{0,1:T(8,128)} fusion(f32[256,64]{0,1:T(8,128)S(1)} %copy.18, f32[64,256]{1,0:T(8,128)} %get-tuple-element.11), kind=kLoop, calls=%fused_computation.17 | loop fusion | flops 16384 | bytes 196608 | tf_op jit(solution)/shard_map/add | solution.py:479
  (3 shorter events, 0.0 us)
Async XLA Ops:
  0.0 41.3 %copy-start = (f32[8,64,64]{2,1,0:T(8,128)S(1)}, f32[8,64,64]{2,1,0:T(8,128)}, u32[]{:S(2)}) copy-start(f32[8,64,64]{2,1,0:T(8,128)} %param.22) | copy-start | bytes 393220
  5.4 0.8 %copy-start.1 = (bf16[256,64]{0,1:T(8,128)(2,1)S(1)}, bf16[256,64]{0,1:T(8,128)(2,1)}, u32[]{:S(2)}) copy-start(bf16[256,64]{0,1:T(8,128)(2,1)} %param.13) | copy-start | bytes 98308
  6.1 0.7 %copy-start.2 = (s32[1,8,16]{2,1,0:T(8,128)S(1)}, s32[1,8,16]{2,1,0:T(8,128)}, u32[]{:S(2)}) copy-start(s32[1,8,16]{2,1,0:T(8,128)} %param.16) | copy-start | bytes 1540
  6.8 0.7 %copy-start.3 = (s32[1,8]{1,0:T(1,128)S(1)}, s32[1,8]{1,0:T(1,128)}, u32[]{:S(2)}) copy-start(s32[1,8]{1,0:T(1,128)} %counts_ref.1) | copy-start | bytes 100
  17.3 0.6 %copy-start.4 = (bf16[192,256]{1,0:T(8,128)(2,1)}, bf16[192,256]{1,0:T(8,128)(2,1)S(1)}, u32[]{:S(2)}) copy-start(bf16[192,256]{1,0:T(8,128)(2,1)S(1)} %get-tuple-element.9.table_ref) | copy-start | bytes 294916
  17.9 0.6 %copy-start.5 = (f32[16,8,128]{2,1,0:T(8,128)}, f32[16,8,128]{2,1,0:T(8,128)S(1)}, u32[]{:S(2)}) copy-start(f32[16,8,128]{2,1,0:T(8,128)S(1)} %get-tuple-element.10) | copy-start | bytes 196612
